TPU v7x, 256 devices: a whole 4x4x8 slice. The times are simulated.
256 devices in a mesh: ctx: 16 (over y_hi, x, core), head: 16 (over y_lo, z).
Axes of the slice: x: 4, y: 4 (y_hi: 2, y_lo: 2; y = y_hi * 2 + y_lo), z: 8, core: 2. Of those that a mesh axis runs over, the one named last changes fastest.
Arguments:
- query_latent: bfloat16 [4096, 1536], P(('ctx', 'head')), may hold values from -6 to 6
- norm_gain: bfloat16 [1536], replicated, may hold values from 0.099609375 to 1.8984375
- kv_latent: bfloat16 [4096, 576], P(('ctx', 'head')), may hold values from -120 to 120
- q_up: bfloat16 [1536, 12288], P(None, 'head'), may hold values from -0.15625 to 0.15625
- absorb_key: bfloat16 [64, 128, 512], P('head'), may hold values from -0.5 to 0.5
- absorb_value: bfloat16 [64, 512, 128], P('head'), may hold values from -0.25 to 0.25
- block_owner: int32 [16], replicated, may hold values from 0 to 15, each once
Outputs:
- head_output: bfloat16 [4096, 8192], P('ctx', 'head')
All inputs are finite; a program needn't handle non-finite values.
Results may differ from a plain program's by a relative error of at most 0.024.
The roundings to bfloat16 on the way count: a program that leaves them out, or rounds other values in their place, can miss the bound.
Values may be sent and summed in bfloat16 or wider, within the bound.
No kernel may reach another device: no remote copies, remote signals or barrier semaphores. Data moves between devices by JAX's collectives and lax.ppermute only.
A program may use at most 64 MiB of HBM per device.

v0:
```python
import math

import jax
import jax.numpy as jnp
from jax import lax
from jax.sharding import PartitionSpec as P

epsilon = 1e-06
masked_score = -1e30


def rotate(values, positions):
    half_width = values.shape[-1] // 2
    frequency = jnp.exp(
        jnp.arange(half_width, dtype=jnp.float32) * (-math.log(10000.0) / half_width)
    )
    angles = positions.astype(jnp.float32)[:, None, None] * frequency
    cosine = jnp.cos(angles)
    sine = jnp.sin(angles)
    front = values[..., :half_width]
    back = values[..., half_width:]
    return jnp.concatenate([front * cosine - back * sine, front * sine + back * cosine], axis=-1)


def per_device(query_latent, norm_gain, kv_latent, q_up, absorb_key, absorb_value, block_owner):
    tok_dev = lax.axis_size("head") * query_latent.shape[0]
    half_len = tok_dev // 2
    ctx_count = lax.axis_size("ctx")
    head_count = absorb_key.shape[0]
    nope_width = absorb_key.shape[1]
    latent_width = absorb_key.shape[2]
    rope_width = q_up.shape[1] // head_count - nope_width
    kv_width = latent_width + rope_width
    score_scale = float(nope_width + rope_width) ** (-0.5)
    ctx_ids = jnp.arange(ctx_count, dtype=jnp.int32)

    def positions_of(row_ids):
        device = row_ids // tok_dev
        owner_ctx = jnp.sum(
            jnp.where(device[:, None] == ctx_ids[None, :], block_owner[None, :], 0), axis=1
        )
        offset = row_ids % tok_dev
        half_block = jnp.where(offset // half_len == 0, owner_ctx, 2 * ctx_count - 1 - owner_ctx)
        return half_block * half_len + offset % half_len

    block_begin = lax.axis_index("ctx") * tok_dev
    query_f32 = query_latent.astype(jnp.float32)
    normed = (
        query_f32
        * lax.rsqrt(jnp.mean(query_f32 * query_f32, axis=-1, keepdims=True) + epsilon)
        * norm_gain.astype(jnp.float32)
    ).astype(jnp.bfloat16)
    row_block = lax.all_gather(normed, "head", axis=0, tiled=True)
    row_count = row_block.shape[0]
    projected = jnp.dot(row_block, q_up, preferred_element_type=jnp.float32)
    projected = projected.reshape(row_count, head_count, nope_width + rope_width)
    q_nope = projected[..., :nope_width].astype(jnp.bfloat16)
    row_places = positions_of(block_begin + jnp.arange(row_count, dtype=jnp.int32))
    q_pe = rotate(projected[..., nope_width:], row_places).astype(jnp.bfloat16)
    q_abs = jnp.einsum(
        "thn,hnc->thc", q_nope, absorb_key, preferred_element_type=jnp.float32
    ).astype(jnp.bfloat16)
    queries = jnp.concatenate([q_abs, q_pe], axis=-1).reshape(row_count * head_count, kv_width)
    query_positions = jnp.repeat(
        positions_of(block_begin + jnp.arange(tok_dev, dtype=jnp.int32)), head_count
    )

    def attend_tile(running, key_rows, key_positions, query_rows, query_places):
        row_peak, row_total, weighted = running
        scores = jnp.dot(query_rows, key_rows.T, preferred_element_type=jnp.float32) * score_scale
        allowed = key_positions[None, :] <= query_places[:, None]
        scores = jnp.where(allowed, scores, masked_score)
        new_peak = jnp.maximum(row_peak, jnp.max(scores, axis=-1))
        weights = jnp.where(allowed, jnp.exp(scores - new_peak[:, None]), 0.0)
        rescale = jnp.exp(row_peak - new_peak)
        row_total = row_total * rescale + jnp.sum(weights, axis=-1)
        weighted = weighted * rescale[:, None] + jnp.dot(
            weights.astype(jnp.bfloat16),
            key_rows[:, :latent_width],
            preferred_element_type=jnp.float32,
        )
        return (new_peak, row_total, weighted)

    def visit(running, key_rows, key_positions):
        return attend_tile(running, key_rows, key_positions, queries, query_positions)

    query_count = tok_dev * head_count
    initial = (
        jnp.full((query_count,), masked_score, jnp.float32),
        jnp.zeros((query_count,), jnp.float32),
        jnp.zeros((query_count, latent_width), jnp.float32),
    )
    group_rows = lax.all_gather(kv_latent, "head", axis=0, tiled=True)
    running = initial
    key_block = lax.all_gather(group_rows, "ctx", axis=0, tiled=True)
    row_count = key_block.shape[0]
    sub_blocks = key_block.reshape(row_count // 256, 256, kv_width)
    block_starts = 256 * jnp.arange(row_count // 256, dtype=jnp.int32)

    def scan_step(state_in, element):
        key_places = positions_of(element[1] + jnp.arange(256, dtype=jnp.int32))
        return (visit(state_in, element[0], key_places), None)

    running, _ = lax.scan(scan_step, running, (sub_blocks, block_starts))
    row_peak, row_total, weighted = running
    latent_out = (
        (weighted / row_total[:, None])
        .astype(jnp.bfloat16)
        .reshape(tok_dev, head_count, latent_width)
    )
    head_output = jnp.einsum(
        "thc,hcv->thv", latent_out, absorb_value, preferred_element_type=jnp.float32
    )
    return head_output.astype(jnp.bfloat16).reshape(tok_dev, head_count * absorb_value.shape[2])


def solution(mesh):
    return jax.shard_map(
        per_device,
        mesh=mesh,
        in_specs=(
            P(("ctx", "head"), None),
            P(),
            P(("ctx", "head"), None),
            P(None, "head"),
            P("head", None, None),
            P("head", None, None),
            P(),
        ),
        out_specs=P("ctx", "head"),
        check_vma=False,
    )
```

profile of v0, /device:TPU:1, one launch (start us, length us, event | category | flops | bytes accessed | tf_op | source)
XLA Modules:
  0.0 279.1 jit_solution(11077566684152425254)
XLA Ops:
  6.5 34.4 %all_gather.9 = bf16[256,576]{1,0:T(8,128)(2,1)} all-gather(bf16[16,576]{1,0:T(8,128)(2,1)} %param.11), channel_id=1, replica_groups=mesh['ctx'=16,'head'=16] {'head'}, dimensions={0}, use_global_device_ids=true | all-gather | bytes 313344 | tf_op jit(solution)/shard_map/all_gather | solution.py:93
  43.5 27.7 %all_gather.11 = bf16[256,1536]{1,0:T(8,128)(2,1)S(1)} all-gather(bf16[16,1536]{1,0:T(8,128)(2,1)S(1)} %fusion.23), channel_id=1, replica_groups=mesh['ctx'=16,'head'=16] {'head'}, dimensions={0}, use_global_device_ids=true | all-gather | bytes 835584 | tf_op jit(solution)/shard_map/all_gather | solution.py:53
  75.5 2.1 copy.34
  77.7 3.4 %reshape.222 = bf16[1024,576]{1,0:T(8,128)(2,1)} reshape(bf16[256,4,576]{2,1,0:T(4,128)(2,1)} %copy.34) | data formatting | bytes 2359296 | tf_op jit(solution)/shard_map/reshape | solution.py:63
  81.1 29.4 %all-gather.2.cloned.1.call-done = bf16[4096,576]{1,0:T(8,128)(2,1)} async-done(((bf16[256,576]{1,0:T(8,128)(2,1)}), bf16[4096,576]{1,0:T(8,128)(2,1)}) %all-gather.2.cloned.1.call-update) | async-done | bytes 4718608 | tf_op jit(solution)/shard_map/all_gather | solution.py:95
  110.4 156.2 %while.18 = (s32[]{:T(128)}, f32[1024]{0:T(1024)S(1)}, f32[1024]{0:T(1024)S(1)}, f32[1024,512]{1,0:T(8,128)}, s32[16]{0:T(128)S(1)}, /*index=5*/s32[16]{0:T(128)...) while((s32[]{:T(128)}, f32[1024]{0:T(1024)S(1)}, ...), condition=%wide.region_6.7_spmd.clone, body=%wide.region_2.6_spmd.clone.sunk | while | flops 575174400 | bytes 9766097 | solution.py:104
  114.2 2.1 fusion.51
  116.6 2.9 %fusion.54 = f32[1024,512]{1,0:T(8,128)} fusion(f32[1024,512]{1,0:T(8,128)} %get-tuple-element.319, f32[1024]{0:T(1024)S(1)} %get-tuple-element.304, pred[]{:T(512)S(6)} %compare.55, f32[1024,256]{0,1:T(8,128)S(1)} %get-tuple-element.302, f32[1024]{0:T(1024)S(1)} %select_maximum_fusion.2, s32[1024]{0:T(1024)S(1)} %le.68, s32[256]{0:T(256)S(1)} %fusion.50, ...), kind=kOutput, calls=%fused_computation.3.clone.1 | convolution fusion | flops 271056896 | bytes 5518337 | tf_op jit(solution)/shard_map/while/body/eval_jaxpr/dot_general | solution.py:77
  125.6 3.7 %fusion.54 = f32[1024,512]{1,0:T(8,128)} fusion(f32[1024,512]{1,0:T(8,128)} %get-tuple-element.319, f32[1024]{0:T(1024)S(1)} %get-tuple-element.304, pred[]{:T(512)S(6)} %compare.55, f32[1024,256]{0,1:T(8,128)S(1)} %get-tuple-element.302, f32[1024]{0:T(1024)S(1)} %select_maximum_fusion.2, s32[1024]{0:T(1024)S(1)} %le.68, s32[256]{0:T(256)S(1)} %fusion.50, ...), kind=kOutput, calls=%fused_computation.3.clone.1 | convolution fusion | flops 271056896 | bytes 5518337 | tf_op jit(solution)/shard_map/while/body/eval_jaxpr/dot_general | solution.py:77
  133.1 2.1 fusion.51
  135.4 3.7 %fusion.54 = f32[1024,512]{1,0:T(8,128)} fusion(f32[1024,512]{1,0:T(8,128)} %get-tuple-element.319, f32[1024]{0:T(1024)S(1)} %get-tuple-element.304, pred[]{:T(512)S(6)} %compare.55, f32[1024,256]{0,1:T(8,128)S(1)} %get-tuple-element.302, f32[1024]{0:T(1024)S(1)} %select_maximum_fusion.2, s32[1024]{0:T(1024)S(1)} %le.68, s32[256]{0:T(256)S(1)} %fusion.50, ...), kind=kOutput, calls=%fused_computation.3.clone.1 | convolution fusion | flops 271056896 | bytes 5518337 | tf_op jit(solution)/shard_map/while/body/eval_jaxpr/dot_general | solution.py:77
  142.9 2.1 fusion.51
  145.2 3.7 %fusion.54 = f32[1024,512]{1,0:T(8,128)} fusion(f32[1024,512]{1,0:T(8,128)} %get-tuple-element.319, f32[1024]{0:T(1024)S(1)} %get-tuple-element.304, pred[]{:T(512)S(6)} %compare.55, f32[1024,256]{0,1:T(8,128)S(1)} %get-tuple-element.302, f32[1024]{0:T(1024)S(1)} %select_maximum_fusion.2, s32[1024]{0:T(1024)S(1)} %le.68, s32[256]{0:T(256)S(1)} %fusion.50, ...), kind=kOutput, calls=%fused_computation.3.clone.1 | convolution fusion | flops 271056896 | bytes 5518337 | tf_op jit(solution)/shard_map/while/body/eval_jaxpr/dot_general | solution.py:77
  152.7 2.1 fusion.51
  155.0 3.7 %fusion.54 = f32[1024,512]{1,0:T(8,128)} fusion(f32[1024,512]{1,0:T(8,128)} %get-tuple-element.319, f32[1024]{0:T(1024)S(1)} %get-tuple-element.304, pred[]{:T(512)S(6)} %compare.55, f32[1024,256]{0,1:T(8,128)S(1)} %get-tuple-element.302, f32[1024]{0:T(1024)S(1)} %select_maximum_fusion.2, s32[1024]{0:T(1024)S(1)} %le.68, s32[256]{0:T(256)S(1)} %fusion.50, ...), kind=kOutput, calls=%fused_computation.3.clone.1 | convolution fusion | flops 271056896 | bytes 5518337 | tf_op jit(solution)/shard_map/while/body/eval_jaxpr/dot_general | solution.py:77
  162.5 2.1 fusion.51
  164.9 3.7 %fusion.54 = f32[1024,512]{1,0:T(8,128)} fusion(f32[1024,512]{1,0:T(8,128)} %get-tuple-element.319, f32[1024]{0:T(1024)S(1)} %get-tuple-element.304, pred[]{:T(512)S(6)} %compare.55, f32[1024,256]{0,1:T(8,128)S(1)} %get-tuple-element.302, f32[1024]{0:T(1024)S(1)} %select_maximum_fusion.2, s32[1024]{0:T(1024)S(1)} %le.68, s32[256]{0:T(256)S(1)} %fusion.50, ...), kind=kOutput, calls=%fused_computation.3.clone.1 | convolution fusion | flops 271056896 | bytes 5518337 | tf_op jit(solution)/shard_map/while/body/eval_jaxpr/dot_general | solution.py:77
  172.3 2.1 fusion.51
  174.7 3.7 %fusion.54 = f32[1024,512]{1,0:T(8,128)} fusion(f32[1024,512]{1,0:T(8,128)} %get-tuple-element.319, f32[1024]{0:T(1024)S(1)} %get-tuple-element.304, pred[]{:T(512)S(6)} %compare.55, f32[1024,256]{0,1:T(8,128)S(1)} %get-tuple-element.302, f32[1024]{0:T(1024)S(1)} %select_maximum_fusion.2, s32[1024]{0:T(1024)S(1)} %le.68, s32[256]{0:T(256)S(1)} %fusion.50, ...), kind=kOutput, calls=%fused_computation.3.clone.1 | convolution fusion | flops 271056896 | bytes 5518337 | tf_op jit(solution)/shard_map/while/body/eval_jaxpr/dot_general | solution.py:77
  182.1 2.1 fusion.51
  184.5 3.7 %fusion.54 = f32[1024,512]{1,0:T(8,128)} fusion(f32[1024,512]{1,0:T(8,128)} %get-tuple-element.319, f32[1024]{0:T(1024)S(1)} %get-tuple-element.304, pred[]{:T(512)S(6)} %compare.55, f32[1024,256]{0,1:T(8,128)S(1)} %get-tuple-element.302, f32[1024]{0:T(1024)S(1)} %select_maximum_fusion.2, s32[1024]{0:T(1024)S(1)} %le.68, s32[256]{0:T(256)S(1)} %fusion.50, ...), kind=kOutput, calls=%fused_computation.3.clone.1 | convolution fusion | flops 271056896 | bytes 5518337 | tf_op jit(solution)/shard_map/while/body/eval_jaxpr/dot_general | solution.py:77
  191.9 2.1 fusion.51
  194.3 3.7 %fusion.54 = f32[1024,512]{1,0:T(8,128)} fusion(f32[1024,512]{1,0:T(8,128)} %get-tuple-element.319, f32[1024]{0:T(1024)S(1)} %get-tuple-element.304, pred[]{:T(512)S(6)} %compare.55, f32[1024,256]{0,1:T(8,128)S(1)} %get-tuple-element.302, f32[1024]{0:T(1024)S(1)} %select_maximum_fusion.2, s32[1024]{0:T(1024)S(1)} %le.68, s32[256]{0:T(256)S(1)} %fusion.50, ...), kind=kOutput, calls=%fused_computation.3.clone.1 | convolution fusion | flops 271056896 | bytes 5518337 | tf_op jit(solution)/shard_map/while/body/eval_jaxpr/dot_general | solution.py:77
  201.8 2.1 fusion.51
  204.1 3.7 %fusion.54 = f32[1024,512]{1,0:T(8,128)} fusion(f32[1024,512]{1,0:T(8,128)} %get-tuple-element.319, f32[1024]{0:T(1024)S(1)} %get-tuple-element.304, pred[]{:T(512)S(6)} %compare.55, f32[1024,256]{0,1:T(8,128)S(1)} %get-tuple-element.302, f32[1024]{0:T(1024)S(1)} %select_maximum_fusion.2, s32[1024]{0:T(1024)S(1)} %le.68, s32[256]{0:T(256)S(1)} %fusion.50, ...), kind=kOutput, calls=%fused_computation.3.clone.1 | convolution fusion | flops 271056896 | bytes 5518337 | tf_op jit(solution)/shard_map/while/body/eval_jaxpr/dot_general | solution.py:77
  211.6 2.1 fusion.51
  213.9 3.7 %fusion.54 = f32[1024,512]{1,0:T(8,128)} fusion(f32[1024,512]{1,0:T(8,128)} %get-tuple-element.319, f32[1024]{0:T(1024)S(1)} %get-tuple-element.304, pred[]{:T(512)S(6)} %compare.55, f32[1024,256]{0,1:T(8,128)S(1)} %get-tuple-element.302, f32[1024]{0:T(1024)S(1)} %select_maximum_fusion.2, s32[1024]{0:T(1024)S(1)} %le.68, s32[256]{0:T(256)S(1)} %fusion.50, ...), kind=kOutput, calls=%fused_computation.3.clone.1 | convolution fusion | flops 271056896 | bytes 5518337 | tf_op jit(solution)/shard_map/while/body/eval_jaxpr/dot_general | solution.py:77
  223.7 3.7 %fusion.54 = f32[1024,512]{1,0:T(8,128)} fusion(f32[1024,512]{1,0:T(8,128)} %get-tuple-element.319, f32[1024]{0:T(1024)S(1)} %get-tuple-element.304, pred[]{:T(512)S(6)} %compare.55, f32[1024,256]{0,1:T(8,128)S(1)} %get-tuple-element.302, f32[1024]{0:T(1024)S(1)} %select_maximum_fusion.2, s32[1024]{0:T(1024)S(1)} %le.68, s32[256]{0:T(256)S(1)} %fusion.50, ...), kind=kOutput, calls=%fused_computation.3.clone.1 | convolution fusion | flops 271056896 | bytes 5518337 | tf_op jit(solution)/shard_map/while/body/eval_jaxpr/dot_general | solution.py:77
  233.5 3.7 %fusion.54 = f32[1024,512]{1,0:T(8,128)} fusion(f32[1024,512]{1,0:T(8,128)} %get-tuple-element.319, f32[1024]{0:T(1024)S(1)} %get-tuple-element.304, pred[]{:T(512)S(6)} %compare.55, f32[1024,256]{0,1:T(8,128)S(1)} %get-tuple-element.302, f32[1024]{0:T(1024)S(1)} %select_maximum_fusion.2, s32[1024]{0:T(1024)S(1)} %le.68, s32[256]{0:T(256)S(1)} %fusion.50, ...), kind=kOutput, calls=%fused_computation.3.clone.1 | convolution fusion | flops 271056896 | bytes 5518337 | tf_op jit(solution)/shard_map/while/body/eval_jaxpr/dot_general | solution.py:77
  243.3 3.7 %fusion.54 = f32[1024,512]{1,0:T(8,128)} fusion(f32[1024,512]{1,0:T(8,128)} %get-tuple-element.319, f32[1024]{0:T(1024)S(1)} %get-tuple-element.304, pred[]{:T(512)S(6)} %compare.55, f32[1024,256]{0,1:T(8,128)S(1)} %get-tuple-element.302, f32[1024]{0:T(1024)S(1)} %select_maximum_fusion.2, s32[1024]{0:T(1024)S(1)} %le.68, s32[256]{0:T(256)S(1)} %fusion.50, ...), kind=kOutput, calls=%fused_computation.3.clone.1 | convolution fusion | flops 271056896 | bytes 5518337 | tf_op jit(solution)/shard_map/while/body/eval_jaxpr/dot_general | solution.py:77
  253.2 3.7 %fusion.54 = f32[1024,512]{1,0:T(8,128)} fusion(f32[1024,512]{1,0:T(8,128)} %get-tuple-element.319, f32[1024]{0:T(1024)S(1)} %get-tuple-element.304, pred[]{:T(512)S(6)} %compare.55, f32[1024,256]{0,1:T(8,128)S(1)} %get-tuple-element.302, f32[1024]{0:T(1024)S(1)} %select_maximum_fusion.2, s32[1024]{0:T(1024)S(1)} %le.68, s32[256]{0:T(256)S(1)} %fusion.50, ...), kind=kOutput, calls=%fused_computation.3.clone.1 | convolution fusion | flops 271056896 | bytes 5518337 | tf_op jit(solution)/shard_map/while/body/eval_jaxpr/dot_general | solution.py:77
  263.0 3.7 %fusion.54 = f32[1024,512]{1,0:T(8,128)} fusion(f32[1024,512]{1,0:T(8,128)} %get-tuple-element.319, f32[1024]{0:T(1024)S(1)} %get-tuple-element.304, pred[]{:T(512)S(6)} %compare.55, f32[1024,256]{0,1:T(8,128)S(1)} %get-tuple-element.302, f32[1024]{0:T(1024)S(1)} %select_maximum_fusion.2, s32[1024]{0:T(1024)S(1)} %le.68, s32[256]{0:T(256)S(1)} %fusion.50, ...), kind=kOutput, calls=%fused_computation.3.clone.1 | convolution fusion | flops 271056896 | bytes 5518337 | tf_op jit(solution)/shard_map/while/body/eval_jaxpr/dot_general | solution.py:77
  (218 shorter events, 89.1 us)
Async XLA Ops:
  6.5 64.7 %copy-start = (bf16[1536,768]{1,0:T(8,128)(2,1)S(1)}, bf16[1536,768]{1,0:T(8,128)(2,1)}, u32[]{:S(2)}) copy-start(bf16[1536,768]{1,0:T(8,128)(2,1)} %param.12) | copy-start | bytes 7077892
  6.5 103.9 %all-gather.2.cloned.1.call-start = ((), (), s32[]{:S(2)}) async-start(), calls=%async_computation | async-start | bytes 5570560 | tf_op jit(solution)/shard_map/all_gather | solution.py:95
  71.2 2.4 copy-start.4
  72.2 0.9 copy-start.1
  73.5 1.1 copy-start.2
  73.5 1.3 copy-start.3
Sparse Core Ops, SparseCore 0:
  41.1 69.2 all-gather.1
where the time goes:
time: 281 us; the launch traced here: 279 us
  matrix products  94.3 us (34%)
  blocking collectives  62.1 us (22%)
  local copies, waits for them, and re-layouts  49.6 us (18%)
  waiting for transfers between devices  29.4 us (10%)
  other arithmetic  29.3 us (10%)
  between operations  13.6 us (5%)
    dot_general x16, matrix products, attend_tile(): jnp.dot(weights.astype(jnp.bfloat16), key_rows[:, :latent_width], preferr...  58 us
    all_gather x1, blocking collectives, per_device(): group_rows = lax.all_gather(kv_latent, 'head', axis=0, tiled=True)  34.4 us
    dot_general x16, matrix products, attend_tile(): jnp.dot(query_rows, key_rows.T, preferred_element_type=jnp.float32)  33 us
    all_gather x1, waiting for transfers between devices, per_device(): key_block = lax.all_gather(group_rows, 'ctx', axis=0, tiled=True)  29.4 us
    squeeze x16, local copies, waits for them, and re-layouts, per_device(): running, _ = lax.scan(scan_step, running, (sub_blocks, block_starts))  27.9 us
    all_gather x1, blocking collectives, per_device(): row_block = lax.all_gather(normed, 'head', axis=0, tiled=True)  27.7 us
    add x16, other arithmetic, positions_of(): return half_block * half_len + offset % half_len  9.36 us
    select_n x17, other arithmetic, positions_of(): device = row_ids // tok_dev  9.18 us
  transfers between devices with their start and end apart: 1, of which 1 were waited for; matrix products, arithmetic and copies ran while one was open for 4% of the time, Pallas kernels for 0%

commit v1 on v0

v1 whole, which is shorter than its diff:
```python
import math

import jax
import jax.numpy as jnp
from jax import lax
from jax.experimental import pallas as pl
from jax.experimental.pallas import tpu as pltpu
from jax.sharding import PartitionSpec as P

QLAT = 1536
LATENT = 512
ROPE = 64
NOPE = 128
KV = LATENT + ROPE
HD = 4
HALF = 128
NB = 32
EPS = 1e-06
SCALE2 = float(NOPE + ROPE) ** (-0.5) * math.log2(math.e)
MASKED = -1e30
AXES = ("ctx", "head")
SHIFTS = (1, 3, 2)


def flat(x, y, z, c):
    x, y, z, c = x % 4, y % 4, z % 8, c % 2
    return (((y // 2) * 4 + x) * 2 + c) * 16 + (y % 2) * 8 + z


def move(a, to):
    pairs = []
    for x in range(4):
        for y in range(4):
            for z in range(8):
                for c in range(2):
                    pairs.append((flat(x, y, z, c), flat(*to(x, y, z, c))))
    return lax.ppermute(a, AXES, pairs)


def shift(k, first):
    def to(x, y, z, c):
        return (x + k, y, z, c) if (c == 0) == first else (x, y + k, z, c)

    return to


def swap_core(x, y, z, c):
    return (x, y, z, c + 1)


def project_kernel(q_ref, gain_ref, cos_ref, sin_ref, up_ref, ak_ref, out_ref):
    x = q_ref[...].astype(jnp.float32)
    ms = jnp.mean(x * x, axis=-1, keepdims=True)
    normed = (x * lax.rsqrt(ms + EPS) * gain_ref[...].astype(jnp.float32)).astype(jnp.bfloat16)
    proj = jnp.dot(normed, up_ref[...], preferred_element_type=jnp.float32)
    cos, sin = cos_ref[...], sin_ref[...]
    for h in range(HD):
        base = h * (NOPE + ROPE)
        nope = proj[:, base : base + NOPE].astype(jnp.bfloat16)
        a = proj[:, base + NOPE : base + NOPE + ROPE // 2]
        b = proj[:, base + NOPE + ROPE // 2 : base + NOPE + ROPE]
        pe = jnp.concatenate([a * cos - b * sin, a * sin + b * cos], axis=-1).astype(jnp.bfloat16)
        qa = jnp.dot(nope, ak_ref[h], preferred_element_type=jnp.float32).astype(jnp.bfloat16)
        for half in range(2):
            r = (half * HD + h) * HALF
            out_ref[r : r + HALF, :LATENT] = qa[half * HALF : (half + 1) * HALF]
            out_ref[r : r + HALF, LATENT:] = pe[half * HALF : (half + 1) * HALF]


def attend_kernel(place_ref, owner_ref, q_ref, av_ref, *rest):
    pieces = rest[:8]
    out_ref = rest[8]
    kv, acc, m_ref, l_ref, sems = rest[9:]
    me_x, me_y, me_c = place_ref[0], place_ref[1], place_ref[2]

    def copy(src, b):
        return pltpu.make_async_copy(
            src, kv.at[pl.ds(pl.multiple_of(b * HALF, HALF), HALF)], sems.at[b]
        )

    offs = (0,) + SHIFTS
    for far in range(2):
        core = me_c if far == 0 else 1 - me_c
        for j in range(4):
            for i in range(4):
                first, second = offs[i], offs[j]
                dx = jnp.where(core == 0, first, second)
                dy = jnp.where(core == 0, second, first)
                x = (me_x - dx + 4) % 4
                y = (me_y - dy + 4) % 4
                p = owner_ref[((y // 2) * 4 + x) * 2 + core]
                b = jnp.where(y % 2 == 0, p, NB - 1 - p)
                copy(pieces[far * 4 + j].at[i * HALF : (i + 1) * HALF], b).start()

    mine = owner_ref[((me_y // 2) * 4 + me_x) * 2 + me_c]

    def wait(b):
        copy(pieces[0].at[0:HALF], b).wait()

    def tile(half, j, masked, a):
        keys = kv[pl.ds(pl.multiple_of(j * 256, 256), 256), :]
        vals = keys[:, :LATENT]
        for g in range(4):
            r = half * 512 + g * HALF
            s = lax.dot_general(
                q_ref[r : r + HALF, :], keys, (((1,), (1,)), ((), ())),
                preferred_element_type=jnp.float32,
            )
            if masked:
                col = lax.broadcasted_iota(jnp.int32, (HALF, 256), 1) + j * 256
                row = lax.broadcasted_iota(jnp.int32, (HALF, 256), 0) + a * HALF
                s = jnp.where(col <= row, s, MASKED)
            rows = slice(g * HALF, (g + 1) * HALF)
            old = m_ref[rows]
            new = jnp.maximum(old, jnp.max(s, axis=-1, keepdims=True))
            w = jnp.exp2((s - new[:, :1]) * SCALE2)
            f = jnp.exp2((old - new) * SCALE2)
            m_ref[rows] = new
            l_ref[rows] = l_ref[rows] * f + (w[:, :128] + w[:, 128:])
            acc[rows] = acc[rows] * f[:, :1] + jnp.dot(
                w.astype(jnp.bfloat16), vals, preferred_element_type=jnp.float32
            )

    seen = 0
    for half in range(2):
        a = mine if half == 0 else NB - 1 - mine
        m_ref[...] = jnp.full_like(m_ref, MASKED)
        l_ref[...] = jnp.zeros_like(l_ref)
        acc[...] = jnp.zeros_like(acc)
        last = a // 2

        def step(j, _):
            @pl.when(j >= seen)
            def _():
                wait(2 * j)
                wait(2 * j + 1)

            tile(half, j, False, a)
            return 0

        lax.fori_loop(0, last, step, 0)

        @pl.when(last >= seen)
        def _():
            wait(2 * last)
            wait(2 * last + 1)

        tile(half, last, True, a)
        seen = last + 1
        for g in range(HD):
            rows = slice(g * HALF, (g + 1) * HALF)
            total = jnp.sum(l_ref[rows], axis=-1, keepdims=True)
            lat = (acc[rows] / total).astype(jnp.bfloat16)
            out_ref[half * HALF : (half + 1) * HALF, g * HALF : (g + 1) * HALF] = jnp.dot(
                lat, av_ref[g], preferred_element_type=jnp.float32
            ).astype(jnp.bfloat16)

    def drain(j, _):
        wait(2 * j)
        wait(2 * j + 1)
        return 0

    lax.fori_loop(seen, NB // 2, drain, 0)


def per_device(query_latent, norm_gain, kv_latent, q_up, absorb_key, absorb_value, block_owner):
    ctx, head = lax.axis_index("ctx"), lax.axis_index("head")
    me_x, me_y, me_c = (ctx // 2) % 4, (ctx // 8) * 2 + head // 8, ctx % 2
    place = jnp.stack([me_x, me_y, me_c]).astype(jnp.int32)

    z_groups = [list(range(8)), list(range(8, 16))]
    own = lax.all_to_all(
        jnp.broadcast_to(kv_latent[None], (8,) + kv_latent.shape),
        "head", 0, 0, axis_index_groups=z_groups, tiled=True,
    ).reshape(HALF, KV)
    ring = jnp.concatenate([own] + [move(own, shift(k, True)) for k in SHIFTS], axis=0)
    mine = [ring] + [move(ring, shift(k, False)) for k in SHIFTS]
    other = [move(t, swap_core) for t in mine]

    rows = lax.all_to_all(
        jnp.broadcast_to(query_latent[None], (16,) + query_latent.shape),
        "head", 0, 0, tiled=True,
    ).reshape(256, QLAT)
    p = block_owner[ctx]
    offset = jnp.arange(256, dtype=jnp.int32)
    pos = jnp.where(offset < HALF, p * HALF + offset, (NB - 1 - p) * HALF + offset - HALF)
    freq = jnp.exp(jnp.arange(ROPE // 2, dtype=jnp.float32) * (-math.log(10000.0) / (ROPE // 2)))
    angles = pos.astype(jnp.float32)[:, None] * freq
    vm = pl.BlockSpec(memory_space=pltpu.VMEM)
    queries = pl.pallas_call(
        project_kernel,
        out_shape=jax.ShapeDtypeStruct((1024, KV), jnp.bfloat16),
        in_specs=[vm] * 6,
        out_specs=vm,
        compiler_params=pltpu.CompilerParams(vmem_limit_bytes=24 * 2**20),
        cost_estimate=pl.CostEstimate(flops=750_000_000, bytes_accessed=5_000_000, transcendentals=0),
    )(rows, norm_gain.reshape(1, QLAT), jnp.cos(angles), jnp.sin(angles), q_up, absorb_key)

    sm = pl.BlockSpec(memory_space=pltpu.SMEM)
    return pl.pallas_call(
        attend_kernel,
        out_shape=jax.ShapeDtypeStruct((256, 512), jnp.bfloat16),
        in_specs=[sm, sm, vm, vm] + [pl.BlockSpec(memory_space=pl.ANY)] * 8,
        out_specs=vm,
        scratch_shapes=[
            pltpu.VMEM((NB * HALF, KV), jnp.bfloat16),
            pltpu.VMEM((512, LATENT), jnp.float32),
            pltpu.VMEM((512, 128), jnp.float32),
            pltpu.VMEM((512, 128), jnp.float32),
            pltpu.SemaphoreType.DMA((NB,)),
        ],
        compiler_params=pltpu.CompilerParams(vmem_limit_bytes=32 * 2**20),
        cost_estimate=pl.CostEstimate(flops=5_000_000_000, bytes_accessed=8_000_000, transcendentals=2_200_000),
    )(place, block_owner, queries, absorb_value, *mine, *other)


def solution(mesh):
    return jax.shard_map(
        per_device,
        mesh=mesh,
        in_specs=(
            P(AXES, None),
            P(),
            P(AXES, None),
            P(None, "head"),
            P("head", None, None),
            P("head", None, None),
            P(),
        ),
        out_specs=P("ctx", "head"),
        check_vma=False,
    )
```

time: 281 us -> 130 us (0.46)
  matrix products: 94.3 us -> 0 us
  Pallas kernels: 0 us -> 47.4 us
  blocking collectives: 62.1 us -> 17 us
  other arithmetic: 29.3 us -> 1.35 us
  local copies, waits for them, and re-layouts: 49.6 us -> 26.8 us
  starting transfers between devices: 0.01 us -> 19 us
  waiting for transfers between devices: 29.4 us -> 16.3 us
  between operations: 13.6 us -> 1.59 us
    dot_general x35 -> x0, matrix products: 94.3 us -> none  [the longest x16 58 us: attend_tile(): jnp.dot(weights.astype(jnp.bfloat16), key_rows[:, :latent_width], preferr...]
    all_gather x2 -> x0, blocking collectives: 62.1 us -> none  [the longest x1 34.4 us: per_device(): group_rows = lax.all_gather(kv_latent, 'head', axis=0, tiled=True)]
    pallas_call x0 -> x2, Pallas kernels: none -> 47.4 us  [the longest x1 45.9 us: per_device(): pl.pallas_call(attend_kernel, out_shape=jax.ShapeDtypeStruct((256, 512),...]
    all_gather x1 -> x0, waiting for transfers between devices: 29.4 us -> none  [per_device(): key_block = lax.all_gather(group_rows, 'ctx', axis=0, tiled=True)]
    squeeze x16 -> x0, local copies, waits for them, and re-layouts: 27.9 us -> none  [per_device(): running, _ = lax.scan(scan_step, running, (sub_blocks, block_starts))]
    all_to_all x0 -> x1, blocking collectives: none -> 17 us  [per_device(): lax.all_to_all(jnp.broadcast_to(kv_latent[None], (8,) + kv_latent.shape),...]
    ppermute x0 -> x10, waiting for transfers between devices: none -> 16.3 us  [move(): return lax.ppermute(a, AXES, pairs)]
    ppermute x0 -> x10, starting transfers between devices: none -> 15.2 us  [move(): return lax.ppermute(a, AXES, pairs)]
  transfers between devices with their start and end apart: 1 -> 11, of which waited for: 1 -> 5; matrix products, arithmetic and copies ran while one was open for 4% -> 10% of each run, Pallas kernels for 0% -> 1%
where the time goes in v1:
time: 130 us; the launch traced here: 129 us
  Pallas kernels  47.4 us (36%)
  local copies, waits for them, and re-layouts  26.8 us (21%)
  starting transfers between devices  19 us (15%)
  blocking collectives  17 us (13%)
  waiting for transfers between devices  16.3 us (13%)
  between operations  1.59 us (1%)
  other arithmetic  1.35 us (1%)
    pallas_call x1, Pallas kernels, per_device(): pl.pallas_call(attend_kernel, out_shape=jax.ShapeDtypeStruct((256, 512),...  45.9 us
    all_to_all x1, blocking collectives, per_device(): lax.all_to_all(jnp.broadcast_to(kv_latent[None], (8,) + kv_latent.shape),...  17 us
    ppermute x10, waiting for transfers between devices, move(): return lax.ppermute(a, AXES, pairs)  16.3 us
    ppermute x10, starting transfers between devices, move(): return lax.ppermute(a, AXES, pairs)  15.2 us
    ppermute x7, local copies, waits for them, and re-layouts, move(): return lax.ppermute(a, AXES, pairs)  13.3 us
    unnamed x24, local copies, waits for them, and re-layouts  10.1 us
    all_to_all x1, starting transfers between devices, per_device(): lax.all_to_all(jnp.broadcast_to(query_latent[None], (16,) + query_latent....  3.79 us
  transfers between devices with their start and end apart: 11, of which 5 were waited for; matrix products, arithmetic and copies ran while one was open for 10% of the time, Pallas kernels for 1%

profile of v1, /device:TPU:1, one launch (start us, length us, event | category | flops | bytes accessed | tf_op | source)
XLA Modules:
  0.0 129.4 jit_solution(4013118432428585680)
XLA Ops:
  0.7 17.0 %all_to_all.10 = bf16[8,16,576]{2,1,0:T(8,128)(2,1)S(1)} all-to-all(bf16[8,16,576]{2,1,0:T(8,128)(2,1)S(1)} %broadcast_in_dim.5), channel_id=1, replica_groups={{0,1,2,3,4,5,6,7},{8,9,10,11,12,13,14,15},{16,17,18,19,20,21,22,23},{24..., dimensions={0} | all-to-all | bytes 294912 | tf_op jit(solution)/shard_map/all_to_all | solution.py:172
  17.7 1.8 %broadcast_in_dim.4 = bf16[16,16,1536]{2,1,0:T(8,128)(2,1)} broadcast(bf16[16,1536]{1,0:T(8,128)(2,1)} %param.7), dimensions={1,2} | broadcast | bytes 835584 | tf_op jit(solution)/shard_map/broadcast_in_dim | solution.py:181
  19.5 3.8 %all-to-all-start = ((bf16[16,16,1536]{2,1,0:T(8,128)(2,1)}), bf16[16,16,1536]{2,1,0:T(8,128)(2,1)S(1)}, u32[]{:S(2)}, u32[]{:S(2)}) async-start(bf16[16,16,1536]{2,1,0:T(8,128)(2,1)} %broadcast_in_dim.4), calls=%async_computation | async-start | bytes 1572864 | tf_op jit(solution)/shard_map/all_to_all | solution.py:180
  23.3 1.4 %collective-permute-start = (bf16[128,576]{1,0:T(8,128)(2,1)S(1)}, bf16[128,576]{1,0:T(8,128)(2,1)S(1)}, u32[]{:S(2)}, u32[]{:S(2)}) collective-permute-start(bf16[128,576]{1,0:T(8,128)(2,1)S(1)} %bitcast.8), channel_id=1, source_target_pairs={{0,32},{16,24},{1,33},{17,25},{2,34},{18,26},{3,35},{19,27},{4,36}... | collective-permute-start | bytes 442376 | tf_op jit(solution)/shard_map/ppermute | solution.py:37
  24.7 1.6 %collective-permute-start.1 = (bf16[128,576]{1,0:T(8,128)(2,1)S(1)}, bf16[128,576]{1,0:T(8,128)(2,1)S(1)}, u32[]{:S(2)}, u32[]{:S(2)}) collective-permute-start(bf16[128,576]{1,0:T(8,128)(2,1)S(1)} %bitcast.9), channel_id=1, source_target_pairs={{0,96},{16,152},{1,97},{17,153},{2,98},{18,154},{3,99},{19,155},{4... | collective-permute-start | bytes 442376 | tf_op jit(solution)/shard_map/ppermute | solution.py:37
  26.3 1.3 collective-permute-start.2
  27.6 1.3 %collective-permute-done = bf16[128,576]{1,0:T(8,128)(2,1)S(1)} collective-permute-done((bf16[128,576]{1,0:T(8,128)(2,1)S(1)}, bf16[128,576]{1,0:T(8,128)(2,1)S(1)}, u32[]{:S(2)}, u32[]{:S(2)}) %collective-permute-start) | collective-permute-done | bytes 147488 | tf_op jit(solution)/shard_map/ppermute | solution.py:37
  28.9 1.9 %collective-permute-done.1 = bf16[128,576]{1,0:T(8,128)(2,1)S(1)} collective-permute-done((bf16[128,576]{1,0:T(8,128)(2,1)S(1)}, bf16[128,576]{1,0:T(8,128)(2,1)S(1)}, u32[]{:S(2)}, u32[]{:S(2)}) %collective-permute-start.1) | collective-permute-done | bytes 147488 | tf_op jit(solution)/shard_map/ppermute | solution.py:37
  30.8 5.2 %collective-permute-done.2 = bf16[128,576]{1,0:T(8,128)(2,1)S(1)} collective-permute-done((bf16[128,576]{1,0:T(8,128)(2,1)S(1)}, bf16[128,576]{1,0:T(8,128)(2,1)S(1)}, u32[]{:S(2)}, u32[]{:S(2)}) %collective-permute-start.2) | collective-permute-done | bytes 147488 | tf_op jit(solution)/shard_map/ppermute | solution.py:37
  36.2 1.3 collective-permute-start.3
  37.5 1.5 %collective-permute-start.4 = (bf16[512,576]{0,1:T(8,128)(2,1)S(1)}, bf16[512,576]{0,1:T(8,128)(2,1)}, u32[]{:S(2)}, u32[]{:S(2)}) collective-permute-start(bf16[512,576]{0,1:T(8,128)(2,1)S(1)} %copy.20), channel_id=1, source_target_pairs={{0,136},{16,112},{1,137},{17,113},{2,138},{18,114},{3,139},{19,115... | collective-permute-start | bytes 1769480 | tf_op jit(solution)/shard_map/ppermute | solution.py:37
  39.0 1.5 %collective-permute-start.5 = (bf16[512,576]{0,1:T(8,128)(2,1)S(1)}, bf16[512,576]{0,1:T(8,128)(2,1)}, u32[]{:S(2)}, u32[]{:S(2)}) collective-permute-start(bf16[512,576]{0,1:T(8,128)(2,1)S(1)} %copy.20), channel_id=1, source_target_pairs={{0,128},{16,80},{1,129},{17,81},{2,130},{18,82},{3,131},{19,83},{4... | collective-permute-start | bytes 1769480 | tf_op jit(solution)/shard_map/ppermute | solution.py:37
  43.4 3.3 %collective-permute-done.3 = bf16[512,576]{0,1:T(8,128)(2,1)} collective-permute-done((bf16[512,576]{0,1:T(8,128)(2,1)S(1)}, bf16[512,576]{0,1:T(8,128)(2,1)}, u32[]{:S(2)}, u32[]{:S(2)}) %collective-permute-start.3) | collective-permute-done | bytes 589856 | tf_op jit(solution)/shard_map/ppermute | solution.py:37
  46.7 1.1 collective-permute-start.7
  47.8 1.5 %collective-permute-start.8 = (bf16[512,576]{0,1:T(8,128)(2,1)}, bf16[512,576]{0,1:T(8,128)(2,1)}, u32[]{:S(2)}, u32[]{:S(2)}) collective-permute-start(bf16[512,576]{0,1:T(8,128)(2,1)} %collective-permute-done.4), channel_id=1, source_target_pairs={{0,16},{16,0},{1,17},{17,1},{2,18},{18,2},{3,19},{19,3},{4,20},{20... | collective-permute-start | bytes 1769480 | tf_op jit(solution)/shard_map/ppermute | solution.py:37
  49.3 4.7 %collective-permute-done.5 = bf16[512,576]{0,1:T(8,128)(2,1)} collective-permute-done((bf16[512,576]{0,1:T(8,128)(2,1)S(1)}, bf16[512,576]{0,1:T(8,128)(2,1)}, u32[]{:S(2)}, u32[]{:S(2)}) %collective-permute-start.5) | collective-permute-done | bytes 589856 | tf_op jit(solution)/shard_map/ppermute | solution.py:37
  54.0 3.1 %collective-permute-start.9 = (bf16[512,576]{0,1:T(8,128)(2,1)}, bf16[512,576]{0,1:T(8,128)(2,1)}, u32[]{:S(2)}, u32[]{:S(2)}) collective-permute-start(bf16[512,576]{0,1:T(8,128)(2,1)} %collective-permute-done.5), channel_id=1, source_target_pairs={{0,16},{16,0},{1,17},{17,1},{2,18},{18,2},{3,19},{19,3},{4,20},{20... | collective-permute-start | bytes 1769480 | tf_op jit(solution)/shard_map/ppermute | solution.py:37
  57.2 1.2 multiply_sine_fusion
  58.4 1.4 %copy.24.rest_1_ = bf16[512,576]{1,0:T(8,128)(2,1)S(1)} copy(bf16[512,576]{0,1:T(8,128)(2,1)} %collective-permute-done.3) | data formatting | bytes 1179648 | tf_op jit(solution)/shard_map/ppermute | solution.py:37
  59.8 2.2 %copy.25.rest_2_ = bf16[512,576]{1,0:T(8,128)(2,1)} copy(bf16[512,576]{0,1:T(8,128)(2,1)} %collective-permute-done.4) | data formatting | bytes 1179648 | tf_op jit(solution)/shard_map/ppermute | solution.py:37
  61.9 2.2 %copy.26.rest_3_ = bf16[512,576]{1,0:T(8,128)(2,1)} copy(bf16[512,576]{0,1:T(8,128)(2,1)} %collective-permute-done.5) | data formatting | bytes 1179648 | tf_op jit(solution)/shard_map/ppermute | solution.py:37
  64.1 1.1 copy.27.rest_4_
  65.2 1.7 %copy-done = bf16[1536,768]{1,0:T(8,128)(2,1)S(1)} copy-done((bf16[1536,768]{1,0:T(8,128)(2,1)S(1)}, bf16[1536,768]{1,0:T(8,128)(2,1)}, u32[]{:S(2)}) %copy-start) | copy-done | bytes 2359320
  68.8 1.5 %shard_map.73.q_ref = bf16[1024,576]{1,0:T(8,128)(2,1)S(1)} custom-call(bf16[256,1536]{1,0:T(8,128)(2,1)S(1)} %bitcast.7, bf16[1,1536]{1,0:T(2,128)(2,1)S(1)} %reshape.34.gain_ref, f32[256,32]{1,0:T(8,128)S(1)} %copy-done.7, f32[256,32]{1,0:T(8,128)S(1)} %get-tuple-element.5.sin_ref, bf16[1536,768]{1,0:T(8,128)(2,1)S(1)} %copy-done, ...), custom_call_target="tpu_custom_call" | custom-call | flops 750000000 | bytes 5000000 | tf_op jit(solution)/shard_map/pallas_call | solution.py:190
  70.3 2.1 %copy.28.rest_5_ = bf16[512,576]{1,0:T(8,128)(2,1)} copy(bf16[512,576]{0,1:T(8,128)(2,1)} %collective-permute-done.7) | data formatting | bytes 1179648 | tf_op jit(solution)/shard_map/ppermute | solution.py:37
  72.5 2.2 %copy.29.rest_6_ = bf16[512,576]{1,0:T(8,128)(2,1)} copy(bf16[512,576]{0,1:T(8,128)(2,1)} %collective-permute-done.8) | data formatting | bytes 1179648 | tf_op jit(solution)/shard_map/ppermute | solution.py:37
  74.7 2.2 %copy.30.rest_7_ = bf16[512,576]{1,0:T(8,128)(2,1)} copy(bf16[512,576]{0,1:T(8,128)(2,1)} %collective-permute-done.9) | data formatting | bytes 1179648 | tf_op jit(solution)/shard_map/ppermute | solution.py:37
  76.9 1.1 copy-done.2
  78.0 1.1 copy-done.3
  79.1 1.1 copy-done.4
  80.2 1.1 copy-done.5
  83.4 45.9 %shard_map.74 = bf16[256,512]{1,0:T(8,128)(2,1)} custom-call(s32[3]{0:T(128)S(1)} %pad_add_fusion.place_ref, s32[16]{0:T(128)S(1)} %copy-done.10, bf16[1024,576]{1,0:T(8,128)(2,1)S(1)} %shard_map.73.q_ref, bf16[4,512,128]{2,1,0:T(8,128)(2,1)S(1)} %copy-done.9, bf16[512,576]{1,0:T(8,128)(2,1)S(1)} %pad_maximum_fusion.rest_0_, ...), custom_call_target="tpu_custom_call" | custom-call | flops 5000000000 | bytes 8000000 | tf_op jit(solution)/shard_map/pallas_call | solution.py:200
  (34 shorter events, 6.7 us)
Async XLA Ops:
  19.5 45.7 %all-to-all-start = ((bf16[16,16,1536]{2,1,0:T(8,128)(2,1)}), bf16[16,16,1536]{2,1,0:T(8,128)(2,1)S(1)}, u32[]{:S(2)}, u32[]{:S(2)}) async-start(bf16[16,16,1536]{2,1,0:T(8,128)(2,1)} %broadcast_in_dim.4), calls=%async_computation | async-start | bytes 1572864 | tf_op jit(solution)/shard_map/all_to_all | solution.py:180
  23.3 18.2 %copy-start.10 = (s32[16]{0:T(128)S(1)}, s32[16]{0:T(128)}, u32[]{:S(2)}) copy-start(s32[16]{0:T(128)} %owner_ref.1) | copy-start | bytes 196
  23.3 20.0 %copy-start.11 = (bf16[1536]{0:T(1024)(128)(2,1)S(1)}, bf16[1536]{0:T(1024)(128)(2,1)}, u32[]{:S(2)}) copy-start(bf16[1536]{0:T(1024)(128)(2,1)} %param.8) | copy-start | bytes 9220
  23.3 5.6 %collective-permute-start = (bf16[128,576]{1,0:T(8,128)(2,1)S(1)}, bf16[128,576]{1,0:T(8,128)(2,1)S(1)}, u32[]{:S(2)}, u32[]{:S(2)}) collective-permute-start(bf16[128,576]{1,0:T(8,128)(2,1)S(1)} %bitcast.8), channel_id=1, source_target_pairs={{0,32},{16,24},{1,33},{17,25},{2,34},{18,26},{3,35},{19,27},{4,36}... | collective-permute-start | bytes 442376 | tf_op jit(solution)/shard_map/ppermute | solution.py:37
  24.7 6.0 %collective-permute-start.1 = (bf16[128,576]{1,0:T(8,128)(2,1)S(1)}, bf16[128,576]{1,0:T(8,128)(2,1)S(1)}, u32[]{:S(2)}, u32[]{:S(2)}) collective-permute-start(bf16[128,576]{1,0:T(8,128)(2,1)S(1)} %bitcast.9), channel_id=1, source_target_pairs={{0,96},{16,152},{1,97},{17,153},{2,98},{18,154},{3,99},{19,155},{4... | collective-permute-start | bytes 442376 | tf_op jit(solution)/shard_map/ppermute | solution.py:37
  26.3 9.6 %collective-permute-start.2 = (bf16[128,576]{1,0:T(8,128)(2,1)S(1)}, bf16[128,576]{1,0:T(8,128)(2,1)S(1)}, u32[]{:S(2)}, u32[]{:S(2)}) collective-permute-start(bf16[128,576]{1,0:T(8,128)(2,1)S(1)} %bitcast.10), channel_id=1, source_target_pairs={{0,64},{16,144},{1,65},{17,145},{2,66},{18,146},{3,67},{19,147},{4... | collective-permute-start | bytes 442376 | tf_op jit(solution)/shard_map/ppermute | solution.py:37
  36.2 10.4 %collective-permute-start.3 = (bf16[512,576]{0,1:T(8,128)(2,1)S(1)}, bf16[512,576]{0,1:T(8,128)(2,1)}, u32[]{:S(2)}, u32[]{:S(2)}) collective-permute-start(bf16[512,576]{0,1:T(8,128)(2,1)S(1)} %copy.20), channel_id=1, source_target_pairs={{0,8},{16,48},{1,9},{17,49},{2,10},{18,50},{3,11},{19,51},{4,12},{... | collective-permute-start | bytes 1769480 | tf_op jit(solution)/shard_map/ppermute | solution.py:37
  37.5 10.2 %collective-permute-start.4 = (bf16[512,576]{0,1:T(8,128)(2,1)S(1)}, bf16[512,576]{0,1:T(8,128)(2,1)}, u32[]{:S(2)}, u32[]{:S(2)}) collective-permute-start(bf16[512,576]{0,1:T(8,128)(2,1)S(1)} %copy.20), channel_id=1, source_target_pairs={{0,136},{16,112},{1,137},{17,113},{2,138},{18,114},{3,139},{19,115... | collective-permute-start | bytes 1769480 | tf_op jit(solution)/shard_map/ppermute | solution.py:37
  39.0 15.0 %collective-permute-start.5 = (bf16[512,576]{0,1:T(8,128)(2,1)S(1)}, bf16[512,576]{0,1:T(8,128)(2,1)}, u32[]{:S(2)}, u32[]{:S(2)}) collective-permute-start(bf16[512,576]{0,1:T(8,128)(2,1)S(1)} %copy.20), channel_id=1, source_target_pairs={{0,128},{16,80},{1,129},{17,81},{2,130},{18,82},{3,131},{19,83},{4... | collective-permute-start | bytes 1769480 | tf_op jit(solution)/shard_map/ppermute | solution.py:37
  40.5 23.5 %collective-permute-start.6 = (bf16[512,576]{0,1:T(8,128)(2,1)S(1)}, bf16[512,576]{0,1:T(8,128)(2,1)S(1)}, u32[]{:S(2)}, u32[]{:S(2)}) collective-permute-start(bf16[512,576]{0,1:T(8,128)(2,1)S(1)} %copy.20), channel_id=1, source_target_pairs={{0,16},{16,0},{1,17},{17,1},{2,18},{18,2},{3,19},{19,3},{4,20},{20... | collective-permute-start | bytes 1769480 | tf_op jit(solution)/shard_map/ppermute | solution.py:37
  46.7 23.7 %collective-permute-start.7 = (bf16[512,576]{0,1:T(8,128)(2,1)}, bf16[512,576]{0,1:T(8,128)(2,1)}, u32[]{:S(2)}, u32[]{:S(2)}) collective-permute-start(bf16[512,576]{0,1:T(8,128)(2,1)} %collective-permute-done.3), channel_id=1, source_target_pairs={{0,16},{16,0},{1,17},{17,1},{2,18},{18,2},{3,19},{19,3},{4,20},{20... | collective-permute-start | bytes 1769480 | tf_op jit(solution)/shard_map/ppermute | solution.py:37
  47.8 24.7 %collective-permute-start.8 = (bf16[512,576]{0,1:T(8,128)(2,1)}, bf16[512,576]{0,1:T(8,128)(2,1)}, u32[]{:S(2)}, u32[]{:S(2)}) collective-permute-start(bf16[512,576]{0,1:T(8,128)(2,1)} %collective-permute-done.4), channel_id=1, source_target_pairs={{0,16},{16,0},{1,17},{17,1},{2,18},{18,2},{3,19},{19,3},{4,20},{20... | collective-permute-start | bytes 1769480 | tf_op jit(solution)/shard_map/ppermute | solution.py:37
  54.0 20.7 %collective-permute-start.9 = (bf16[512,576]{0,1:T(8,128)(2,1)}, bf16[512,576]{0,1:T(8,128)(2,1)}, u32[]{:S(2)}, u32[]{:S(2)}) collective-permute-start(bf16[512,576]{0,1:T(8,128)(2,1)} %collective-permute-done.5), channel_id=1, source_target_pairs={{0,16},{16,0},{1,17},{17,1},{2,18},{18,2},{3,19},{19,3},{4,20},{20... | collective-permute-start | bytes 1769480 | tf_op jit(solution)/shard_map/ppermute | solution.py:37
  65.2 1.7 %copy-start = (bf16[1536,768]{1,0:T(8,128)(2,1)S(1)}, bf16[1536,768]{1,0:T(8,128)(2,1)}, u32[]{:S(2)}) copy-start(bf16[1536,768]{1,0:T(8,128)(2,1)} %up_ref.1) | copy-start | bytes 7077892
  66.9 0.9 copy-start.7
  67.8 1.0 copy-start.8
  72.5 4.4 %copy-start.1 = (bf16[512,576]{1,0:T(8,128)(2,1)S(1)}, bf16[512,576]{1,0:T(8,128)(2,1)}, u32[]{:S(2)}) copy-start(bf16[512,576]{1,0:T(8,128)(2,1)} %copy.25.rest_2_) | copy-start | bytes 1769476
  76.9 1.1 copy-start.2
  78.0 1.1 copy-start.3
  79.1 1.1 copy-start.4
  80.2 1.1 copy-start.5
  81.2 1.1 copy-start.6
  82.3 1.0 copy-start.9

commit v2 on v1

v2 whole, which is shorter than its diff:
```python
import functools
import math

import jax
import jax.numpy as jnp
from jax import lax
from jax.experimental import pallas as pl
from jax.experimental.pallas import tpu as pltpu
from jax.sharding import PartitionSpec as P

QLAT = 1536
LATENT = 512
ROPE = 64
NOPE = 128
KV = LATENT + ROPE
HD = 4
HALF = 128
NB = 32
EPS = 1e-06
SCALE2 = float(NOPE + ROPE) ** (-0.5) * math.log2(math.e)
MASKED = -1e30
AXES = ("ctx", "head")
SHIFTS = (1, 3, 2)


def flat(x, y, z, c):
    x, y, z, c = x % 4, y % 4, z % 8, c % 2
    return (((y // 2) * 4 + x) * 2 + c) * 16 + (y % 2) * 8 + z


def move(a, to):
    pairs = []
    for x in range(4):
        for y in range(4):
            for z in range(8):
                for c in range(2):
                    pairs.append((flat(x, y, z, c), flat(*to(x, y, z, c))))
    return lax.ppermute(a, AXES, pairs)


def shift(k, first):
    def to(x, y, z, c):
        return (x + k, y, z, c) if (c == 0) == first else (x, y + k, z, c)

    return to


def swap_core(x, y, z, c):
    return (x, y, z, c + 1)


def turn_kernel(x_ref, out_ref):
    out_ref[...] = x_ref[...].reshape(HALF, KV).T


def project_kernel(q_ref, gain_ref, cos_ref, sin_ref, up_ref, ak_ref, out_ref):
    x = q_ref[...].astype(jnp.float32)
    ms = jnp.mean(x * x, axis=-1, keepdims=True)
    normed = (x * lax.rsqrt(ms + EPS) * gain_ref[...].astype(jnp.float32)).astype(jnp.bfloat16)
    proj = lax.dot_general(
        up_ref[...], normed, (((0,), (1,)), ((), ())), preferred_element_type=jnp.float32
    )
    cos, sin = cos_ref[...], sin_ref[...]
    for h in range(HD):
        base = h * (NOPE + ROPE)
        nope = proj[base : base + NOPE].astype(jnp.bfloat16)
        a = proj[base + NOPE : base + NOPE + ROPE // 2]
        b = proj[base + NOPE + ROPE // 2 : base + NOPE + ROPE]
        pe = jnp.concatenate([a * cos - b * sin, a * sin + b * cos], axis=0).astype(jnp.bfloat16)
        qa = lax.dot_general(
            ak_ref[h], nope, (((0,), (0,)), ((), ())), preferred_element_type=jnp.float32
        ).astype(jnp.bfloat16)
        for half in range(2):
            cols = slice(h * HALF, (h + 1) * HALF)
            out_ref[half, :LATENT, cols] = qa[:, half * HALF : (half + 1) * HALF]
            out_ref[half, LATENT:, cols] = pe[:, half * HALF : (half + 1) * HALF]


def attend_kernel(slots, first, last, place_ref, owner_ref, q_ref, *rest):
    rest = list(rest)
    if last:
        av_ref = rest.pop(0)
    if not first:
        acc_in, m_in, l_in = rest.pop(0), rest.pop(0), rest.pop(0)
    pieces = [rest.pop(0) for _ in slots]
    if last:
        out_ref = rest.pop(0)
        keys, acc, m_ref, l_ref, s_now, s_next, rank, bpos = rest
    else:
        acc, m_ref, l_ref = rest.pop(0), rest.pop(0), rest.pop(0)
        keys, s_now, s_next, rank, bpos = rest
    me_x, me_y, me_c = place_ref[0], place_ref[1], place_ref[2]

    where = []
    for b in range(NB):
        rank[b] = 0
    for far, second in slots:
        core = me_c if far == 0 else 1 - me_c
        for i in range(4):
            along = (0,) + SHIFTS
            dx = jnp.where(core == 0, along[i], second)
            dy = jnp.where(core == 0, second, along[i])
            x = (me_x - dx + 4) & 3
            y = (me_y - dy + 4) & 3
            p = owner_ref[(y >> 1) * 8 + x * 2 + core]
            b = jnp.where((y & 1) == 0, p, NB - 1 - p)
            rank[b] = 1
            where.append(b)
    mine = owner_ref[(me_y >> 1) * 8 + me_x * 2 + me_c]
    other = NB - 1 - mine
    count = jnp.int32(0)
    low = jnp.int32(0)
    high = jnp.int32(0)
    for b in range(NB):
        here = rank[b]
        rank[b] = count
        bpos[count] = b
        count = count + here
        low = low + jnp.where(b <= mine, here, 0)
        high = high + jnp.where(b <= other, here, 0)
    for s, b in enumerate(where):
        keys[rank[b]] = pieces[s // 4][s % 4]

    if first:
        acc[...] = jnp.zeros_like(acc)
        m_ref[...] = jnp.full_like(m_ref, MASKED)
        l_ref[...] = jnp.zeros_like(l_ref)
    else:
        acc[...] = acc_in[...]
        m_ref[...] = m_in[...]
        l_ref[...] = l_in[...]

    tiles_high = (high + 3) // 4
    tiles = tiles_high + (low + 3) // 4
    delta = (
        lax.broadcasted_iota(jnp.int32, (HALF, 512), 0)
        - (lax.broadcasted_iota(jnp.int32, (HALF, 512), 1) & (HALF - 1))
    )

    def at(t):
        is_high = t < tiles_high
        half = jnp.where(is_high, 1, 0)
        return half, jnp.where(is_high, t, t - tiles_high), jnp.where(is_high, other, mine)

    def load(j):
        return jnp.concatenate([keys[4 * j + i] for i in range(4)], axis=1)

    def score(t):
        half, j, a = at(t)
        s = lax.dot_general(
            load(j), q_ref[half], (((0,), (0,)), ((), ())), preferred_element_type=jnp.float32
        )
        return jnp.concatenate(
            [
                jnp.where(
                    delta <= (a - bpos[4 * j + i]) * HALF, s[i * HALF : (i + 1) * HALF], MASKED
                )
                for i in range(4)
            ],
            axis=0,
        )

    def update(t, s):
        half, j, _ = at(t)
        old = m_ref[half]
        new = jnp.maximum(old, jnp.max(s, axis=0, keepdims=True))
        w = jnp.exp2((s - new) * SCALE2)
        f = jnp.exp2((old - new) * SCALE2)
        m_ref[half] = new
        l_ref[half] = l_ref[half] * f + jnp.sum(w, axis=0, keepdims=True)
        acc[half] = acc[half] * f + jnp.dot(
            load(j)[:LATENT], w.astype(jnp.bfloat16), preferred_element_type=jnp.float32
        )

    @pl.when(tiles > 0)
    def _():
        s_now[...] = score(0)

    def step(t, _):
        s_next[...] = score(jnp.minimum(t + 1, tiles - 1))
        update(t, s_now[...])
        s_now[...] = s_next[...]
        return 0

    lax.fori_loop(0, tiles, step, 0)

    if last:
        for half in range(2):
            for h in range(HD):
                cols = slice(h * HALF, (h + 1) * HALF)
                lat = (acc[half, :, cols] / l_ref[half, :, cols]).astype(jnp.bfloat16)
                out_ref[half * HALF : (half + 1) * HALF, cols] = lax.dot_general(
                    lat, av_ref[h], (((0,), (0,)), ((), ())), preferred_element_type=jnp.float32
                ).astype(jnp.bfloat16)


VM = pl.BlockSpec(memory_space=pltpu.VMEM)
SM = pl.BlockSpec(memory_space=pltpu.SMEM)


def attend(place, block_owner, queries, pieces, slots, state=None, value=None):
    first, last = state is None, value is not None
    n = 4 * len(pieces)
    state_shapes = ((2, LATENT, 512), (2, 1, 512), (2, 1, 512))
    scratch = [pltpu.VMEM((n, KV, HALF), jnp.bfloat16)]
    if last:
        scratch += [pltpu.VMEM(s, jnp.float32) for s in state_shapes]
        out = jax.ShapeDtypeStruct((256, 512), jnp.bfloat16)
    else:
        out = [jax.ShapeDtypeStruct(s, jnp.float32) for s in state_shapes]
    scratch += [pltpu.VMEM((512, 512), jnp.float32)] * 2
    scratch += [pltpu.SMEM((NB,), jnp.int32), pltpu.SMEM((NB + 1,), jnp.int32)]
    args = [place, block_owner, queries]
    args += [value] if last else []
    args += [] if first else list(state)
    args += pieces
    return pl.pallas_call(
        functools.partial(attend_kernel, slots, first, last),
        out_shape=out,
        in_specs=[SM, SM] + [VM] * (len(args) - 2),
        out_specs=VM if last else [VM] * 3,
        scratch_shapes=scratch,
        compiler_params=pltpu.CompilerParams(vmem_limit_bytes=30 * 2**20),
        cost_estimate=pl.CostEstimate(
            flops=n * 150_000_000, bytes_accessed=n * 150_000, transcendentals=n * 70_000
        ),
    )(*args)


def per_device(query_latent, norm_gain, kv_latent, q_up, absorb_key, absorb_value, block_owner):
    ctx, head = lax.axis_index("ctx"), lax.axis_index("head")
    me_x, me_y, me_c = (ctx // 2) % 4, (ctx // 8) * 2 + head // 8, ctx % 2
    place = jnp.stack([me_x, me_y, me_c]).astype(jnp.int32)

    z_groups = [list(range(8)), list(range(8, 16))]
    own = lax.all_to_all(
        jnp.broadcast_to(kv_latent[None], (8,) + kv_latent.shape),
        "head", 0, 0, axis_index_groups=z_groups, tiled=True,
    )
    own = pl.pallas_call(
        turn_kernel,
        out_shape=jax.ShapeDtypeStruct((KV, HALF), jnp.bfloat16),
        in_specs=[VM],
        out_specs=VM,
    )(own)
    ring = jnp.stack([own] + [move(own, shift(k, True)) for k in SHIFTS], axis=0)
    near = [ring] + [move(ring, shift(k, False)) for k in SHIFTS]
    distant = [move(t, swap_core) for t in near]

    rows = lax.all_to_all(
        jnp.broadcast_to(query_latent[None], (16,) + query_latent.shape),
        "head", 0, 0, tiled=True,
    ).reshape(256, QLAT)
    p = block_owner[ctx]
    offset = jnp.arange(256, dtype=jnp.int32)
    pos = jnp.where(offset < HALF, p * HALF + offset, (NB - 1 - p) * HALF + offset - HALF)
    freq = jnp.exp(jnp.arange(ROPE // 2, dtype=jnp.float32) * (-math.log(10000.0) / (ROPE // 2)))
    angles = freq[:, None] * pos.astype(jnp.float32)
    queries = pl.pallas_call(
        project_kernel,
        out_shape=jax.ShapeDtypeStruct((2, KV, 512), jnp.bfloat16),
        in_specs=[VM] * 6,
        out_specs=VM,
        compiler_params=pltpu.CompilerParams(vmem_limit_bytes=24 * 2**20),
        cost_estimate=pl.CostEstimate(flops=750_000_000, bytes_accessed=5_000_000, transcendentals=0),
    )(rows, norm_gain.reshape(1, QLAT), jnp.cos(angles), jnp.sin(angles), q_up, absorb_key)

    shifts = (0,) + SHIFTS
    slots = tuple((far, k) for far in range(2) for k in shifts)
    return attend(place, block_owner, queries, near + distant, slots, value=absorb_value)


def solution(mesh):
    return jax.shard_map(
        per_device,
        mesh=mesh,
        in_specs=(
            P(AXES, None),
            P(),
            P(AXES, None),
            P(None, "head"),
            P("head", None, None),
            P("head", None, None),
            P(),
        ),
        out_specs=P("ctx", "head"),
        check_vma=False,
    )
```

time: 130 us -> 75.8 us (0.58)
  Pallas kernels: 47.4 us -> 16.5 us
  local copies, waits for them, and re-layouts: 26.8 us -> 4.3 us
  starting transfers between devices: 19 us -> 17.7 us
    pallas_call x2 -> x3, Pallas kernels: 47.4 us -> 16.5 us  [the longest x1 13 us: attend(): pl.pallas_call(functools.partial(attend_kernel, slots, first, last), out_...]
    ppermute x7 -> x0, local copies, waits for them, and re-layouts: 13.3 us -> none  [move(): return lax.ppermute(a, AXES, pairs)]
    unnamed x24 -> x10, local copies, waits for them, and re-layouts: 10.1 us -> 1.05 us
    another operation x0 -> x1, other arithmetic: none -> 1.81 us  [per_device(): jnp.stack([own] + [move(own, shift(k, True)) for k in SHIFTS], axis=0)]
  transfers between devices with their start and end apart: 11 -> 11, of which waited for: 5 -> 6; matrix products, arithmetic and copies ran while one was open for 10% -> 4% of each run, Pallas kernels for 1% -> 5%
where the time goes in v2:
time: 75.8 us; the launch traced here: 75.4 us
  starting transfers between devices  17.7 us (23%)
  blocking collectives  17.1 us (23%)
  Pallas kernels  16.5 us (22%)
  waiting for transfers between devices  16.3 us (22%)
  local copies, waits for them, and re-layouts  4.3 us (6%)
  other arithmetic  2.1 us (3%)
  between operations  1.45 us (2%)
    all_to_all x1, blocking collectives, per_device(): lax.all_to_all(jnp.broadcast_to(kv_latent[None], (8,) + kv_latent.shape),...  17.1 us
    ppermute x10, waiting for transfers between devices, move(): return lax.ppermute(a, AXES, pairs)  16.3 us
    ppermute x10, starting transfers between devices, move(): return lax.ppermute(a, AXES, pairs)  13.9 us
    pallas_call x1, Pallas kernels, attend(): pl.pallas_call(functools.partial(attend_kernel, slots, first, last), out_...  13 us
    all_to_all x1, starting transfers between devices, per_device(): lax.all_to_all(jnp.broadcast_to(query_latent[None], (16,) + query_latent....  3.79 us
    another operation x1, other arithmetic, per_device(): jnp.stack([own] + [move(own, shift(k, True)) for k in SHIFTS], axis=0)  1.81 us
    pallas_call x1, Pallas kernels, per_device(): pl.pallas_call(project_kernel, out_shape=jax.ShapeDtypeStruct((2, KV, 512...  1.79 us
    broadcast_in_dim x1, local copies, waits for them, and re-layouts, per_device(): jnp.broadcast_to(query_latent[None], (16,) + query_latent.shape)  1.77 us
  transfers between devices with their start and end apart: 11, of which 6 were waited for; matrix products, arithmetic and copies ran while one was open for 4% of the time, Pallas kernels for 5%

profile of v2, /device:TPU:1, one launch (start us, length us, event | category | flops | bytes accessed | tf_op | source)
XLA Modules:
  0.0 75.4 jit_solution(1624439193626031572)
XLA Ops:
  0.0 0.9 %broadcast_in_dim.5 = bf16[8,16,576]{2,1,0:T(8,128)(2,1)S(1)} broadcast(bf16[16,576]{1,0:T(8,128)(2,1)} %param.9), dimensions={1,2} | broadcast | bytes 165888 | tf_op jit(solution)/shard_map/broadcast_in_dim | solution.py:237
  0.9 17.1 %all_to_all.10.x_ref = bf16[8,16,576]{2,1,0:T(8,128)(2,1)} all-to-all(bf16[8,16,576]{2,1,0:T(8,128)(2,1)S(1)} %broadcast_in_dim.5), channel_id=1, replica_groups={{0,1,2,3,4,5,6,7},{8,9,10,11,12,13,14,15},{16,17,18,19,20,21,22,23},{24..., dimensions={0} | all-to-all | bytes 294912 | tf_op jit(solution)/shard_map/all_to_all | solution.py:236
  18.0 1.8 %broadcast_in_dim.4 = bf16[16,16,1536]{2,1,0:T(8,128)(2,1)} broadcast(bf16[16,1536]{1,0:T(8,128)(2,1)} %param.7), dimensions={1,2} | broadcast | bytes 835584 | tf_op jit(solution)/shard_map/broadcast_in_dim | solution.py:251
  19.7 3.8 %all-to-all-start = ((bf16[16,16,1536]{2,1,0:T(8,128)(2,1)}), bf16[16,16,1536]{2,1,0:T(8,128)(2,1)S(1)}, u32[]{:S(2)}, u32[]{:S(2)}) async-start(bf16[16,16,1536]{2,1,0:T(8,128)(2,1)} %broadcast_in_dim.4), calls=%async_computation | async-start | bytes 1572864 | tf_op jit(solution)/shard_map/all_to_all | solution.py:250
  23.5 1.7 %shard_map.74 = bf16[576,128]{1,0:T(8,128)(2,1)} custom-call(bf16[8,16,576]{2,1,0:T(8,128)(2,1)} %all_to_all.10.x_ref), custom_call_target="tpu_custom_call" | custom-call | tf_op jit(solution)/shard_map/pallas_call | solution.py:240
  25.2 1.4 %collective-permute-start = (bf16[576,128]{1,0:T(8,128)(2,1)}, bf16[576,128]{1,0:T(8,128)(2,1)S(1)}, u32[]{:S(2)}, u32[]{:S(2)}) collective-permute-start(bf16[576,128]{1,0:T(8,128)(2,1)} %shard_map.74), channel_id=1, source_target_pairs={{0,32},{16,24},{1,33},{17,25},{2,34},{18,26},{3,35},{19,27},{4,36}... | collective-permute-start | bytes 442376 | tf_op jit(solution)/shard_map/ppermute | solution.py:38
  26.6 1.5 %collective-permute-start.1 = (bf16[576,128]{1,0:T(8,128)(2,1)}, bf16[576,128]{1,0:T(8,128)(2,1)S(1)}, u32[]{:S(2)}, u32[]{:S(2)}) collective-permute-start(bf16[576,128]{1,0:T(8,128)(2,1)} %shard_map.74), channel_id=1, source_target_pairs={{0,96},{16,152},{1,97},{17,153},{2,98},{18,154},{3,99},{19,155},{4... | collective-permute-start | bytes 442376 | tf_op jit(solution)/shard_map/ppermute | solution.py:38
  28.1 1.4 %collective-permute-start.2 = (bf16[576,128]{1,0:T(8,128)(2,1)}, bf16[576,128]{1,0:T(8,128)(2,1)S(1)}, u32[]{:S(2)}, u32[]{:S(2)}) collective-permute-start(bf16[576,128]{1,0:T(8,128)(2,1)} %shard_map.74), channel_id=1, source_target_pairs={{0,64},{16,144},{1,65},{17,145},{2,66},{18,146},{3,67},{19,147},{4... | collective-permute-start | bytes 442376 | tf_op jit(solution)/shard_map/ppermute | solution.py:38
  29.4 1.4 %collective-permute-done = bf16[576,128]{1,0:T(8,128)(2,1)S(1)} collective-permute-done((bf16[576,128]{1,0:T(8,128)(2,1)}, bf16[576,128]{1,0:T(8,128)(2,1)S(1)}, u32[]{:S(2)}, u32[]{:S(2)}) %collective-permute-start) | collective-permute-done | bytes 147488 | tf_op jit(solution)/shard_map/ppermute | solution.py:38
  30.8 1.8 %collective-permute-done.1 = bf16[576,128]{1,0:T(8,128)(2,1)S(1)} collective-permute-done((bf16[576,128]{1,0:T(8,128)(2,1)}, bf16[576,128]{1,0:T(8,128)(2,1)S(1)}, u32[]{:S(2)}, u32[]{:S(2)}) %collective-permute-start.1) | collective-permute-done | bytes 147488 | tf_op jit(solution)/shard_map/ppermute | solution.py:38
  32.6 4.6 %collective-permute-done.2 = bf16[576,128]{1,0:T(8,128)(2,1)S(1)} collective-permute-done((bf16[576,128]{1,0:T(8,128)(2,1)}, bf16[576,128]{1,0:T(8,128)(2,1)S(1)}, u32[]{:S(2)}, u32[]{:S(2)}) %collective-permute-start.2) | collective-permute-done | bytes 147488 | tf_op jit(solution)/shard_map/ppermute | solution.py:38
  37.2 1.8 %pad_maximum_fusion.rest_1_ = bf16[4,576,128]{2,1,0:T(8,128)(2,1)} fusion(bf16[1,576,128]{2,1,0:T(8,128)(2,1)S(1)} %bitcast.14, bf16[1,576,128]{2,1,0:T(8,128)(2,1)S(1)} %bitcast.13, bf16[1,576,128]{2,1,0:T(8,128)(2,1)S(1)} %bitcast.12, bf16[1,576,128]{2,1,0:T(8,128)(2,1)} %bitcast.11), kind=kLoop, calls=%fused_computation | loop fusion | flops 884736 | bytes 1179648 | tf_op jit(solution)/shard_map/stack | solution.py:246
  39.1 1.2 %collective-permute-start.3 = (bf16[4,576,128]{2,1,0:T(8,128)(2,1)}, bf16[4,576,128]{2,1,0:T(8,128)(2,1)}, u32[]{:S(2)}, u32[]{:S(2)}) collective-permute-start(bf16[4,576,128]{2,1,0:T(8,128)(2,1)} %pad_maximum_fusion.rest_1_), channel_id=1, source_target_pairs={{0,8},{16,48},{1,9},{17,49},{2,10},{18,50},{3,11},{19,51},{4,12},{... | collective-permute-start | bytes 1769480 | tf_op jit(solution)/shard_map/ppermute | solution.py:38
  40.3 1.5 %collective-permute-start.4 = (bf16[4,576,128]{2,1,0:T(8,128)(2,1)}, bf16[4,576,128]{2,1,0:T(8,128)(2,1)}, u32[]{:S(2)}, u32[]{:S(2)}) collective-permute-start(bf16[4,576,128]{2,1,0:T(8,128)(2,1)} %pad_maximum_fusion.rest_1_), channel_id=1, source_target_pairs={{0,136},{16,112},{1,137},{17,113},{2,138},{18,114},{3,139},{19,115... | collective-permute-start | bytes 1769480 | tf_op jit(solution)/shard_map/ppermute | solution.py:38
  41.7 1.5 %collective-permute-start.5 = (bf16[4,576,128]{2,1,0:T(8,128)(2,1)}, bf16[4,576,128]{2,1,0:T(8,128)(2,1)}, u32[]{:S(2)}, u32[]{:S(2)}) collective-permute-start(bf16[4,576,128]{2,1,0:T(8,128)(2,1)} %pad_maximum_fusion.rest_1_), channel_id=1, source_target_pairs={{0,128},{16,80},{1,129},{17,81},{2,130},{18,82},{3,131},{19,83},{4... | collective-permute-start | bytes 1769480 | tf_op jit(solution)/shard_map/ppermute | solution.py:38
  43.3 0.6 dynamic_slice.3
  45.2 1.6 %collective-permute-start.6 = (bf16[4,576,128]{2,1,0:T(8,128)(2,1)}, bf16[4,576,128]{2,1,0:T(8,128)(2,1)}, u32[]{:S(2)}, u32[]{:S(2)}) collective-permute-start(bf16[4,576,128]{2,1,0:T(8,128)(2,1)} %pad_maximum_fusion.rest_1_), channel_id=1, source_target_pairs={{0,16},{16,0},{1,17},{17,1},{2,18},{18,2},{3,19},{19,3},{4,20},{20... | collective-permute-start | bytes 1769480 | tf_op jit(solution)/shard_map/ppermute | solution.py:38
  46.8 2.8 %collective-permute-done.3.rest_2_ = bf16[4,576,128]{2,1,0:T(8,128)(2,1)} collective-permute-done((bf16[4,576,128]{2,1,0:T(8,128)(2,1)}, bf16[4,576,128]{2,1,0:T(8,128)(2,1)}, u32[]{:S(2)}, u32[]{:S(2)}) %collective-permute-start.3) | collective-permute-done | bytes 589856 | tf_op jit(solution)/shard_map/ppermute | solution.py:38
  49.6 1.7 %collective-permute-start.7 = (bf16[4,576,128]{2,1,0:T(8,128)(2,1)}, bf16[4,576,128]{2,1,0:T(8,128)(2,1)}, u32[]{:S(2)}, u32[]{:S(2)}) collective-permute-start(bf16[4,576,128]{2,1,0:T(8,128)(2,1)} %collective-permute-done.3.rest_2_), channel_id=1, source_target_pairs={{0,16},{16,0},{1,17},{17,1},{2,18},{18,2},{3,19},{19,3},{4,20},{20... | collective-permute-start | bytes 1769480 | tf_op jit(solution)/shard_map/ppermute | solution.py:38
  51.3 3.9 %collective-permute-done.4.rest_3_ = bf16[4,576,128]{2,1,0:T(8,128)(2,1)} collective-permute-done((bf16[4,576,128]{2,1,0:T(8,128)(2,1)}, bf16[4,576,128]{2,1,0:T(8,128)(2,1)}, u32[]{:S(2)}, u32[]{:S(2)}) %collective-permute-start.4) | collective-permute-done | bytes 589856 | tf_op jit(solution)/shard_map/ppermute | solution.py:38
  55.2 0.0 collective-permute-start.8
  55.2 1.7 %collective-permute-done.5.rest_4_ = bf16[4,576,128]{2,1,0:T(8,128)(2,1)} collective-permute-done((bf16[4,576,128]{2,1,0:T(8,128)(2,1)}, bf16[4,576,128]{2,1,0:T(8,128)(2,1)}, u32[]{:S(2)}, u32[]{:S(2)}) %collective-permute-start.5) | collective-permute-done | bytes 589856 | tf_op jit(solution)/shard_map/ppermute | solution.py:38
  56.9 2.3 %collective-permute-start.9 = (bf16[4,576,128]{2,1,0:T(8,128)(2,1)}, bf16[4,576,128]{2,1,0:T(8,128)(2,1)}, u32[]{:S(2)}, u32[]{:S(2)}) collective-permute-start(bf16[4,576,128]{2,1,0:T(8,128)(2,1)} %collective-permute-done.5.rest_4_), channel_id=1, source_target_pairs={{0,16},{16,0},{1,17},{17,1},{2,18},{18,2},{3,19},{19,3},{4,20},{20... | collective-permute-start | bytes 1769480 | tf_op jit(solution)/shard_map/ppermute | solution.py:38
  59.2 0.1 pad_add_fusion.place_ref
  59.3 0.2 multiply_sine_fusion
  59.5 0.0 all-to-all-done
  59.5 0.0 copy-start.1
  59.6 1.0 %copy-done.1 = bf16[4,128,512]{2,1,0:T(8,128)(2,1)S(1)} copy-done((bf16[4,128,512]{2,1,0:T(8,128)(2,1)S(1)}, bf16[4,128,512]{2,1,0:T(8,128)(2,1)}, u32[]{:S(2)}) %copy-start.1) | copy-done | bytes 524312
  60.6 1.8 %shard_map.73.q_ref = bf16[2,576,512]{2,1,0:T(8,128)(2,1)S(1)} custom-call(bf16[256,1536]{1,0:T(8,128)(2,1)S(1)} %bitcast.10, bf16[1,1536]{1,0:T(2,128)(2,1)S(1)} %reshape.31.gain_ref, f32[32,256]{1,0:T(8,128)S(1)} %get-tuple-element.6.cos_ref, f32[32,256]{1,0:T(8,128)S(1)} %get-tuple-element.5.sin_ref, bf16[1536,768]{1,0:T(8,128)(2,1)S(1)} %copy-done, ...), custom_call_target="tpu_custom_call" | custom-call | flops 750000000 | bytes 5000000 | tf_op jit(solution)/shard_map/pallas_call | solution.py:259
  62.4 0.0 collective-permute-done.6.rest_5_
  62.4 0.0 collective-permute-done.7.rest_6_
  62.4 13.0 %shard_map.75 = bf16[256,512]{1,0:T(8,128)(2,1)} custom-call(s32[3]{0:T(128)S(1)} %pad_add_fusion.place_ref, s32[16]{0:T(128)S(1)} %copy-done.3, bf16[2,576,512]{2,1,0:T(8,128)(2,1)S(1)} %shard_map.73.q_ref, bf16[4,512,128]{2,1,0:T(8,128)(2,1)S(1)} %copy-done.2, bf16[4,576,128]{2,1,0:T(8,128)(2,1)} %pad_maximum_fusion.rest_1_, ...), custom_call_target="tpu_custom_call" | custom-call | flops 4800000000 | bytes 4800000 | tf_op jit(solution)/shard_map/pallas_call | solution.py:217
  (13 shorter events, 0.0 us)
Async XLA Ops:
  0.0 43.3 %copy-start.3 = (s32[16]{0:T(128)S(1)}, s32[16]{0:T(128)}, u32[]{:S(2)}) copy-start(s32[16]{0:T(128)} %owner_ref.1) | copy-start | bytes 196
  0.0 45.2 %copy-start.4 = (bf16[1536]{0:T(1024)(128)(2,1)S(1)}, bf16[1536]{0:T(1024)(128)(2,1)}, u32[]{:S(2)}) copy-start(bf16[1536]{0:T(1024)(128)(2,1)} %param.8) | copy-start | bytes 9220
  0.0 59.5 %copy-start = (bf16[1536,768]{1,0:T(8,128)(2,1)S(1)}, bf16[1536,768]{1,0:T(8,128)(2,1)}, u32[]{:S(2)}) copy-start(bf16[1536,768]{1,0:T(8,128)(2,1)} %up_ref.1) | copy-start | bytes 7077892
  19.7 39.8 %all-to-all-start = ((bf16[16,16,1536]{2,1,0:T(8,128)(2,1)}), bf16[16,16,1536]{2,1,0:T(8,128)(2,1)S(1)}, u32[]{:S(2)}, u32[]{:S(2)}) async-start(bf16[16,16,1536]{2,1,0:T(8,128)(2,1)} %broadcast_in_dim.4), calls=%async_computation | async-start | bytes 1572864 | tf_op jit(solution)/shard_map/all_to_all | solution.py:250
  25.2 5.6 %collective-permute-start = (bf16[576,128]{1,0:T(8,128)(2,1)}, bf16[576,128]{1,0:T(8,128)(2,1)S(1)}, u32[]{:S(2)}, u32[]{:S(2)}) collective-permute-start(bf16[576,128]{1,0:T(8,128)(2,1)} %shard_map.74), channel_id=1, source_target_pairs={{0,32},{16,24},{1,33},{17,25},{2,34},{18,26},{3,35},{19,27},{4,36}... | collective-permute-start | bytes 442376 | tf_op jit(solution)/shard_map/ppermute | solution.py:38
  26.6 6.1 %collective-permute-start.1 = (bf16[576,128]{1,0:T(8,128)(2,1)}, bf16[576,128]{1,0:T(8,128)(2,1)S(1)}, u32[]{:S(2)}, u32[]{:S(2)}) collective-permute-start(bf16[576,128]{1,0:T(8,128)(2,1)} %shard_map.74), channel_id=1, source_target_pairs={{0,96},{16,152},{1,97},{17,153},{2,98},{18,154},{3,99},{19,155},{4... | collective-permute-start | bytes 442376 | tf_op jit(solution)/shard_map/ppermute | solution.py:38
  28.1 9.2 %collective-permute-start.2 = (bf16[576,128]{1,0:T(8,128)(2,1)}, bf16[576,128]{1,0:T(8,128)(2,1)S(1)}, u32[]{:S(2)}, u32[]{:S(2)}) collective-permute-start(bf16[576,128]{1,0:T(8,128)(2,1)} %shard_map.74), channel_id=1, source_target_pairs={{0,64},{16,144},{1,65},{17,145},{2,66},{18,146},{3,67},{19,147},{4... | collective-permute-start | bytes 442376 | tf_op jit(solution)/shard_map/ppermute | solution.py:38
  39.1 10.6 %collective-permute-start.3 = (bf16[4,576,128]{2,1,0:T(8,128)(2,1)}, bf16[4,576,128]{2,1,0:T(8,128)(2,1)}, u32[]{:S(2)}, u32[]{:S(2)}) collective-permute-start(bf16[4,576,128]{2,1,0:T(8,128)(2,1)} %pad_maximum_fusion.rest_1_), channel_id=1, source_target_pairs={{0,8},{16,48},{1,9},{17,49},{2,10},{18,50},{3,11},{19,51},{4,12},{... | collective-permute-start | bytes 1769480 | tf_op jit(solution)/shard_map/ppermute | solution.py:38
  40.3 15.0 %collective-permute-start.4 = (bf16[4,576,128]{2,1,0:T(8,128)(2,1)}, bf16[4,576,128]{2,1,0:T(8,128)(2,1)}, u32[]{:S(2)}, u32[]{:S(2)}) collective-permute-start(bf16[4,576,128]{2,1,0:T(8,128)(2,1)} %pad_maximum_fusion.rest_1_), channel_id=1, source_target_pairs={{0,136},{16,112},{1,137},{17,113},{2,138},{18,114},{3,139},{19,115... | collective-permute-start | bytes 1769480 | tf_op jit(solution)/shard_map/ppermute | solution.py:38
  41.7 15.2 %collective-permute-start.5 = (bf16[4,576,128]{2,1,0:T(8,128)(2,1)}, bf16[4,576,128]{2,1,0:T(8,128)(2,1)}, u32[]{:S(2)}, u32[]{:S(2)}) collective-permute-start(bf16[4,576,128]{2,1,0:T(8,128)(2,1)} %pad_maximum_fusion.rest_1_), channel_id=1, source_target_pairs={{0,128},{16,80},{1,129},{17,81},{2,130},{18,82},{3,131},{19,83},{4... | collective-permute-start | bytes 1769480 | tf_op jit(solution)/shard_map/ppermute | solution.py:38
  45.2 17.2 %collective-permute-start.6 = (bf16[4,576,128]{2,1,0:T(8,128)(2,1)}, bf16[4,576,128]{2,1,0:T(8,128)(2,1)}, u32[]{:S(2)}, u32[]{:S(2)}) collective-permute-start(bf16[4,576,128]{2,1,0:T(8,128)(2,1)} %pad_maximum_fusion.rest_1_), channel_id=1, source_target_pairs={{0,16},{16,0},{1,17},{17,1},{2,18},{18,2},{3,19},{19,3},{4,20},{20... | collective-permute-start | bytes 1769480 | tf_op jit(solution)/shard_map/ppermute | solution.py:38
  49.6 12.8 %collective-permute-start.7 = (bf16[4,576,128]{2,1,0:T(8,128)(2,1)}, bf16[4,576,128]{2,1,0:T(8,128)(2,1)}, u32[]{:S(2)}, u32[]{:S(2)}) collective-permute-start(bf16[4,576,128]{2,1,0:T(8,128)(2,1)} %collective-permute-done.3.rest_2_), channel_id=1, source_target_pairs={{0,16},{16,0},{1,17},{17,1},{2,18},{18,2},{3,19},{19,3},{4,20},{20... | collective-permute-start | bytes 1769480 | tf_op jit(solution)/shard_map/ppermute | solution.py:38
  55.2 7.2 %collective-permute-start.8 = (bf16[4,576,128]{2,1,0:T(8,128)(2,1)}, bf16[4,576,128]{2,1,0:T(8,128)(2,1)}, u32[]{:S(2)}, u32[]{:S(2)}) collective-permute-start(bf16[4,576,128]{2,1,0:T(8,128)(2,1)} %collective-permute-done.4.rest_3_), channel_id=1, source_target_pairs={{0,16},{16,0},{1,17},{17,1},{2,18},{18,2},{3,19},{19,3},{4,20},{20... | collective-permute-start | bytes 1769480 | tf_op jit(solution)/shard_map/ppermute | solution.py:38
  56.9 5.5 %collective-permute-start.9 = (bf16[4,576,128]{2,1,0:T(8,128)(2,1)}, bf16[4,576,128]{2,1,0:T(8,128)(2,1)}, u32[]{:S(2)}, u32[]{:S(2)}) collective-permute-start(bf16[4,576,128]{2,1,0:T(8,128)(2,1)} %collective-permute-done.5.rest_4_), channel_id=1, source_target_pairs={{0,16},{16,0},{1,17},{17,1},{2,18},{18,2},{3,19},{19,3},{4,20},{20... | collective-permute-start | bytes 1769480 | tf_op jit(solution)/shard_map/ppermute | solution.py:38
  59.5 1.0 %copy-start.1 = (bf16[4,128,512]{2,1,0:T(8,128)(2,1)S(1)}, bf16[4,128,512]{2,1,0:T(8,128)(2,1)}, u32[]{:S(2)}) copy-start(bf16[4,128,512]{2,1,0:T(8,128)(2,1)} %ak_ref.1) | copy-start | bytes 1572868
  60.6 1.8 %copy-start.2 = (bf16[4,512,128]{2,1,0:T(8,128)(2,1)S(1)}, bf16[4,512,128]{2,1,0:T(8,128)(2,1)}, u32[]{:S(2)}) copy-start(bf16[4,512,128]{2,1,0:T(8,128)(2,1)} %rest_0_.1) | copy-start | bytes 1572868

commit v3 on v2

--- a/solution.py
+++ b/solution.py
@@ -49,8 +49,17 @@
     return (x, y, z, c + 1)
 
 
-def turn_kernel(x_ref, out_ref):
-    out_ref[...] = x_ref[...].reshape(HALF, KV).T
+def spread_kernel(q_ref, q_out):
+    q_out[...] = jnp.broadcast_to(q_ref[...][None], q_out.shape)
+
+
+def turn_kernel(*refs):
+    for i in range(4):
+        refs[4][i] = refs[i][...].T
+
+
+def gate_kernel(_x, _token, _out):
+    pass
 
 
 def project_kernel(q_ref, gain_ref, cos_ref, sin_ref, up_ref, ak_ref, out_ref):
@@ -79,25 +88,32 @@
 def attend_kernel(slots, first, last, place_ref, owner_ref, q_ref, *rest):
     rest = list(rest)
     if last:
-        av_ref = rest.pop(0)
+        av_src = rest.pop(0)
     if not first:
-        acc_in, m_in, l_in = rest.pop(0), rest.pop(0), rest.pop(0)
+        state = [rest.pop(0) for _ in range(3)]
     pieces = [rest.pop(0) for _ in slots]
     if last:
         out_ref = rest.pop(0)
-        keys, acc, m_ref, l_ref, s_now, s_next, rank, bpos = rest
     else:
-        acc, m_ref, l_ref = rest.pop(0), rest.pop(0), rest.pop(0)
-        keys, s_now, s_next, rank, bpos = rest
+        state = [rest.pop(0) for _ in range(3)]
+    keys = rest.pop(0)
+    if first and last:
+        state = [rest.pop(0) for _ in range(3)]
+    acc, m_ref, l_ref = state
+    s_now, s_next, rank, bpos = rest[:4]
+    if last:
+        av_ref, av_sem = rest[4:]
+        av_copy = pltpu.make_async_copy(av_src, av_ref, av_sem)
+        av_copy.start()
     me_x, me_y, me_c = place_ref[0], place_ref[1], place_ref[2]
 
     where = []
     for b in range(NB):
         rank[b] = 0
+    along = (0,) + SHIFTS
     for far, second in slots:
         core = me_c if far == 0 else 1 - me_c
         for i in range(4):
-            along = (0,) + SHIFTS
             dx = jnp.where(core == 0, along[i], second)
             dy = jnp.where(core == 0, second, along[i])
             x = (me_x - dx + 4) & 3
@@ -125,10 +141,6 @@
         acc[...] = jnp.zeros_like(acc)
         m_ref[...] = jnp.full_like(m_ref, MASKED)
         l_ref[...] = jnp.zeros_like(l_ref)
-    else:
-        acc[...] = acc_in[...]
-        m_ref[...] = m_in[...]
-        l_ref[...] = l_in[...]
 
     tiles_high = (high + 3) // 4
     tiles = tiles_high + (low + 3) // 4
@@ -185,6 +197,7 @@
     lax.fori_loop(0, tiles, step, 0)
 
     if last:
+        av_copy.wait()
         for half in range(2):
             for h in range(HD):
                 cols = slice(h * HALF, (h + 1) * HALF)
@@ -196,6 +209,19 @@
 
 VM = pl.BlockSpec(memory_space=pltpu.VMEM)
 SM = pl.BlockSpec(memory_space=pltpu.SMEM)
+FREE = pl.BlockSpec(memory_space=pl.ANY)
+
+
+def after(x, token):
+    return pl.pallas_call(
+        gate_kernel,
+        out_shape=jax.ShapeDtypeStruct(x.shape, x.dtype),
+        in_specs=[FREE, FREE],
+        out_specs=FREE,
+        input_output_aliases={0: 0},
+        compiler_params=pltpu.CompilerParams(vmem_limit_bytes=2**20),
+        cost_estimate=pl.CostEstimate(flops=1000, bytes_accessed=1000, transcendentals=0),
+    )(x, token)
 
 
 def attend(place, block_owner, queries, pieces, slots, state=None, value=None):
@@ -203,26 +229,34 @@
     n = 4 * len(pieces)
     state_shapes = ((2, LATENT, 512), (2, 1, 512), (2, 1, 512))
     scratch = [pltpu.VMEM((n, KV, HALF), jnp.bfloat16)]
-    if last:
+    aliases = {}
+    if last and first:
         scratch += [pltpu.VMEM(s, jnp.float32) for s in state_shapes]
+    if last:
         out = jax.ShapeDtypeStruct((256, 512), jnp.bfloat16)
     else:
         out = [jax.ShapeDtypeStruct(s, jnp.float32) for s in state_shapes]
     scratch += [pltpu.VMEM((512, 512), jnp.float32)] * 2
     scratch += [pltpu.SMEM((NB,), jnp.int32), pltpu.SMEM((NB + 1,), jnp.int32)]
+    if last:
+        scratch += [pltpu.VMEM((HD, LATENT, 128), jnp.bfloat16), pltpu.SemaphoreType.DMA]
+    specs = [SM, SM, VM] + ([FREE] if last else [])
     args = [place, block_owner, queries]
     args += [value] if last else []
+    if not (first or last):
+        aliases = {len(args) + i: i for i in range(3)}
     args += [] if first else list(state)
     args += pieces
     return pl.pallas_call(
         functools.partial(attend_kernel, slots, first, last),
         out_shape=out,
-        in_specs=[SM, SM] + [VM] * (len(args) - 2),
+        in_specs=specs + [VM] * (len(args) - len(specs)),
         out_specs=VM if last else [VM] * 3,
         scratch_shapes=scratch,
-        compiler_params=pltpu.CompilerParams(vmem_limit_bytes=30 * 2**20),
+        input_output_aliases=aliases,
+        compiler_params=pltpu.CompilerParams(vmem_limit_bytes=16 * 2**20),
         cost_estimate=pl.CostEstimate(
-            flops=n * 150_000_000, bytes_accessed=n * 150_000, transcendentals=n * 70_000
+            flops=n * 1_000_000, bytes_accessed=n * 1_000, transcendentals=0
         ),
     )(*args)
 
@@ -232,25 +266,32 @@
     me_x, me_y, me_c = (ctx // 2) % 4, (ctx // 8) * 2 + head // 8, ctx % 2
     place = jnp.stack([me_x, me_y, me_c]).astype(jnp.int32)
 
-    z_groups = [list(range(8)), list(range(8, 16))]
+    q_spread = pl.pallas_call(
+        spread_kernel,
+        out_shape=jax.ShapeDtypeStruct((16,) + query_latent.shape, jnp.bfloat16),
+        in_specs=[VM],
+        out_specs=VM,
+        compiler_params=pltpu.CompilerParams(vmem_limit_bytes=4 * 2**20),
+    )(query_latent)
+
     own = lax.all_to_all(
         jnp.broadcast_to(kv_latent[None], (8,) + kv_latent.shape),
-        "head", 0, 0, axis_index_groups=z_groups, tiled=True,
-    )
-    own = pl.pallas_call(
+        "head", 0, 0, axis_index_groups=[list(range(8)), list(range(8, 16))], tiled=True
+    ).reshape(HALF, KV)
+
+    rows = lax.all_to_all(q_spread, "head", 0, 0, tiled=True).reshape(256, QLAT)
+
+    blocks = [own] + [move(own, shift(k, True)) for k in SHIFTS]
+    stack = pl.pallas_call(
         turn_kernel,
-        out_shape=jax.ShapeDtypeStruct((KV, HALF), jnp.bfloat16),
-        in_specs=[VM],
+        out_shape=jax.ShapeDtypeStruct((4, KV, HALF), jnp.bfloat16),
+        in_specs=[VM] * 4,
         out_specs=VM,
-    )(own)
-    ring = jnp.stack([own] + [move(own, shift(k, True)) for k in SHIFTS], axis=0)
-    near = [ring] + [move(ring, shift(k, False)) for k in SHIFTS]
-    distant = [move(t, swap_core) for t in near]
-
-    rows = lax.all_to_all(
-        jnp.broadcast_to(query_latent[None], (16,) + query_latent.shape),
-        "head", 0, 0, tiled=True,
-    ).reshape(256, QLAT)
+        compiler_params=pltpu.CompilerParams(vmem_limit_bytes=8 * 2**20),
+    )(*blocks)
+    near = {0: stack}
+    for k in SHIFTS:
+        near[k] = move(stack, shift(k, False))
     p = block_owner[ctx]
     offset = jnp.arange(256, dtype=jnp.int32)
     pos = jnp.where(offset < HALF, p * HALF + offset, (NB - 1 - p) * HALF + offset - HALF)
@@ -261,13 +302,22 @@
         out_shape=jax.ShapeDtypeStruct((2, KV, 512), jnp.bfloat16),
         in_specs=[VM] * 6,
         out_specs=VM,
-        compiler_params=pltpu.CompilerParams(vmem_limit_bytes=24 * 2**20),
+        compiler_params=pltpu.CompilerParams(vmem_limit_bytes=16 * 2**20),
         cost_estimate=pl.CostEstimate(flops=750_000_000, bytes_accessed=5_000_000, transcendentals=0),
     )(rows, norm_gain.reshape(1, QLAT), jnp.cos(angles), jnp.sin(angles), q_up, absorb_key)
 
-    shifts = (0,) + SHIFTS
-    slots = tuple((far, k) for far in range(2) for k in shifts)
-    return attend(place, block_owner, queries, near + distant, slots, value=absorb_value)
+    distant = {0: move(stack, swap_core)}
+
+    def part(keys, **more):
+        pieces = [near[k] for k in keys] + [distant[k] for k in keys]
+        kinds = tuple((far, k) for far in range(2) for k in keys)
+        return attend(place, block_owner, queries, pieces, kinds, **more)
+
+    state = part([0])
+    for k in SHIFTS:
+        near[k] = after(near[k], state[1])
+        distant[k] = move(near[k], swap_core)
+    return part([1, 3, 2], state=state, value=absorb_value)
 
 
 def solution(mesh):

time: 75.8 us -> 72.3 us (0.954)
  the two profiles are of different devices: /device:TPU:1 before, /device:TPU:57 now
where the time goes in v3:
time: 72.3 us; the launch traced here: 72.1 us
  starting transfers between devices  37 us (51%)
  Pallas kernels  17.6 us (24%)
  waiting for transfers between devices  10.2 us (14%)
  local copies, waits for them, and re-layouts  5.53 us (8%)
  between operations  1.46 us (2%)
    ppermute x10, starting transfers between devices, move(): return lax.ppermute(a, AXES, pairs)  24.5 us
    pallas_call x2, Pallas kernels, attend(): pl.pallas_call(functools.partial(attend_kernel, slots, first, last), out_...  14.6 us
    all_to_all x1, starting transfers between devices, per_device(): lax.all_to_all(jnp.broadcast_to(kv_latent[None], (8,) + kv_latent.shape),...  8.01 us
    all_to_all x1, waiting for transfers between devices, per_device(): lax.all_to_all(jnp.broadcast_to(kv_latent[None], (8,) + kv_latent.shape),...  5.51 us
    ppermute x10, waiting for transfers between devices, move(): return lax.ppermute(a, AXES, pairs)  4.68 us
    all_to_all x1, starting transfers between devices, per_device(): rows = lax.all_to_all(q_spread, 'head', 0, 0, tiled=True).reshape(256, QLAT)  4.53 us
    unnamed x12, local copies, waits for them, and re-layouts  3.51 us
    pallas_call x1, Pallas kernels, per_device(): pl.pallas_call(project_kernel, out_shape=jax.ShapeDtypeStruct((2, KV, 512...  1.8 us
  transfers between devices with their start and end apart: 12, of which 6 were waited for; matrix products, arithmetic and copies ran while one was open for 1% of the time, Pallas kernels for 11%

profile of v3, /device:TPU:57, one launch (start us, length us, event | category | flops | bytes accessed | tf_op | source)
XLA Modules:
  0.0 72.1 jit_solution(11159793293865529369)
XLA Ops:
  0.0 1.4 %broadcast_in_dim.2 = bf16[8,16,576]{2,1,0:T(8,128)(2,1)} broadcast(bf16[16,576]{1,0:T(8,128)(2,1)} %param.9), dimensions={1,2} | broadcast | bytes 165888 | tf_op jit(solution)/shard_map/broadcast_in_dim | solution.py:278
  1.4 8.0 %all-to-all-start.1 = ((bf16[8,16,576]{2,1,0:T(8,128)(2,1)}), bf16[8,16,576]{2,1,0:T(8,128)(2,1)S(1)}, u32[]{:S(2)}, u32[]{:S(2)}) async-start(bf16[8,16,576]{2,1,0:T(8,128)(2,1)} %broadcast_in_dim.2), calls=%async_computation.1 | async-start | bytes 327680 | tf_op jit(solution)/shard_map/all_to_all | solution.py:277
  9.4 0.8 %copy-done.3 = bf16[16,1536]{1,0:T(8,128)(2,1)S(1)} copy-done((bf16[16,1536]{1,0:T(8,128)(2,1)S(1)}, bf16[16,1536]{1,0:T(8,128)(2,1)}, u32[]{:S(2)}) %copy-start.3) | copy-done | bytes 49176
  10.2 1.0 %shard_map.73 = bf16[16,16,1536]{2,1,0:T(8,128)(2,1)} custom-call(bf16[16,1536]{1,0:T(8,128)(2,1)S(1)} %copy-done.3), custom_call_target="tpu_custom_call" | custom-call | tf_op jit(solution)/shard_map/pallas_call | solution.py:269
  11.2 5.5 %all-to-all-done.1 = bf16[8,16,576]{2,1,0:T(8,128)(2,1)S(1)} async-done(((bf16[8,16,576]{2,1,0:T(8,128)(2,1)}), bf16[8,16,576]{2,1,0:T(8,128)(2,1)S(1)}, u32[]{:S(2)}, u32[]{:S(2)}) %all-to-all-start.1) | async-done | bytes 147488 | tf_op jit(solution)/shard_map/all_to_all | solution.py:277
  16.7 4.5 %all-to-all-start = ((bf16[16,16,1536]{2,1,0:T(8,128)(2,1)}), bf16[16,16,1536]{2,1,0:T(8,128)(2,1)S(1)}, u32[]{:S(2)}, u32[]{:S(2)}) async-start(bf16[16,16,1536]{2,1,0:T(8,128)(2,1)} %shard_map.73), calls=%async_computation | async-start | bytes 1572864 | tf_op jit(solution)/shard_map/all_to_all | solution.py:282
  21.2 0.9 %collective-permute-start.2 = (bf16[128,576]{1,0:T(8,128)(2,1)S(1)}, bf16[128,576]{1,0:T(8,128)(2,1)S(1)}, u32[]{:S(2)}, u32[]{:S(2)}) collective-permute-start(bf16[128,576]{1,0:T(8,128)(2,1)S(1)} %bitcast.8), channel_id=1, source_target_pairs={{0,64},{16,144},{1,65},{17,145},{2,66},{18,146},{3,67},{19,147},{4... | collective-permute-start | bytes 442376 | tf_op jit(solution)/shard_map/ppermute | solution.py:38
  22.1 2.7 %collective-permute-start = (bf16[128,576]{1,0:T(8,128)(2,1)S(1)}, bf16[128,576]{1,0:T(8,128)(2,1)S(1)}, u32[]{:S(2)}, u32[]{:S(2)}) collective-permute-start(bf16[128,576]{1,0:T(8,128)(2,1)S(1)} %bitcast.10), channel_id=1, source_target_pairs={{0,32},{16,24},{1,33},{17,25},{2,34},{18,26},{3,35},{19,27},{4,36}... | collective-permute-start | bytes 442376 | tf_op jit(solution)/shard_map/ppermute | solution.py:38
  24.8 0.6 dynamic_slice.3
  26.8 1.5 %collective-permute-done.2.refs_3_ = bf16[128,576]{1,0:T(8,128)(2,1)S(1)} collective-permute-done((bf16[128,576]{1,0:T(8,128)(2,1)S(1)}, bf16[128,576]{1,0:T(8,128)(2,1)S(1)}, u32[]{:S(2)}, u32[]{:S(2)}) %collective-permute-start.2) | collective-permute-done | bytes 147488 | tf_op jit(solution)/shard_map/ppermute | solution.py:38
  28.2 0.7 collective-permute-done.1.refs_2_
  29.0 0.1 collective-permute-done.refs_1_
  29.1 0.2 shard_map.75.rest_0_
  29.3 2.8 %collective-permute-start.6 = (bf16[4,576,128]{2,1,0:T(8,128)(2,1)S(1)}, bf16[4,576,128]{2,1,0:T(8,128)(2,1)S(1)}, u32[]{:S(2)}, u32[]{:S(2)}) collective-permute-start(bf16[4,576,128]{2,1,0:T(8,128)(2,1)S(1)} %shard_map.75.rest_0_), channel_id=1, source_target_pairs={{0,128},{16,80},{1,129},{17,81},{2,130},{18,82},{3,131},{19,83},{4... | collective-permute-start | bytes 1769480 | tf_op jit(solution)/shard_map/ppermute | solution.py:38
  32.1 0.9 %collective-permute-start.5 = (bf16[4,576,128]{2,1,0:T(8,128)(2,1)S(1)}, bf16[4,576,128]{2,1,0:T(8,128)(2,1)S(1)}, u32[]{:S(2)}, u32[]{:S(2)}) collective-permute-start(bf16[4,576,128]{2,1,0:T(8,128)(2,1)S(1)} %shard_map.75.rest_0_), channel_id=1, source_target_pairs={{0,136},{16,112},{1,137},{17,113},{2,138},{18,114},{3,139},{19,115... | collective-permute-start | bytes 1769480 | tf_op jit(solution)/shard_map/ppermute | solution.py:38
  33.0 0.6 collective-permute-start.4
  33.6 11.8 %collective-permute-start.3 = (bf16[4,576,128]{2,1,0:T(8,128)(2,1)S(1)}, bf16[4,576,128]{2,1,0:T(8,128)(2,1)}, u32[]{:S(2)}, u32[]{:S(2)}) collective-permute-start(bf16[4,576,128]{2,1,0:T(8,128)(2,1)S(1)} %shard_map.75.rest_0_), channel_id=1, source_target_pairs={{0,16},{16,0},{1,17},{17,1},{2,18},{18,2},{3,19},{19,3},{4,20},{20... | collective-permute-start | bytes 1769480 | tf_op jit(solution)/shard_map/ppermute | solution.py:38
  45.4 0.1 pad_add_fusion.place_ref
  45.5 0.2 multiply_sine_fusion
  45.7 0.0 copy-start
  45.7 1.7 %copy-done = bf16[1536,768]{1,0:T(8,128)(2,1)S(1)} copy-done((bf16[1536,768]{1,0:T(8,128)(2,1)S(1)}, bf16[1536,768]{1,0:T(8,128)(2,1)}, u32[]{:S(2)}) %copy-start) | copy-done | bytes 2359320
  47.4 1.0 %copy-done.2 = bf16[4,128,512]{2,1,0:T(8,128)(2,1)S(1)} copy-done((bf16[4,128,512]{2,1,0:T(8,128)(2,1)S(1)}, bf16[4,128,512]{2,1,0:T(8,128)(2,1)}, u32[]{:S(2)}) %copy-start.2) | copy-done | bytes 524312
  48.4 1.8 %shard_map.74.q_ref = bf16[2,576,512]{2,1,0:T(8,128)(2,1)S(1)} custom-call(bf16[256,1536]{1,0:T(8,128)(2,1)S(1)} %bitcast.7, bf16[1,1536]{1,0:T(2,128)(2,1)S(1)} %reshape.33.gain_ref, f32[32,256]{1,0:T(8,128)S(1)} %get-tuple-element.12.cos_ref, f32[32,256]{1,0:T(8,128)S(1)} %get-tuple-element.11.sin_ref, bf16[1536,768]{1,0:T(8,128)(2,1)S(1)} %copy-done, ...), custom_call_target="tpu_custom_call" | custom-call | flops 750000000 | bytes 5000000 | tf_op jit(solution)/shard_map/pallas_call | solution.py:300
  50.2 4.6 %shard_map.76 = (f32[2,512,512]{2,1,0:T(8,128)S(1)}, f32[2,1,512]{2,1,0:T(1,128)S(1)}, f32[2,1,512]{2,1,0:T(1,128)S(1)}) custom-call(s32[3]{0:T(128)S(1)} %pad_add_fusion.place_ref, s32[16]{0:T(128)S(1)} %copy-done.4, bf16[2,576,512]{2,1,0:T(8,128)(2,1)S(1)} %shard_map.74.q_ref, bf16[4,576,128]{2,1,0:T(8,128)(2,1)S(1)} %shard_map.75.rest_0_, ...), custom_call_target="tpu_custom_call" | custom-call | flops 8000000 | bytes 8000 | tf_op jit(solution)/shard_map/pallas_call | solution.py:250
  54.8 0.0 copy-start.1
  54.8 0.0 collective-permute-done.4._x
  54.9 0.1 collective-permute-start.7
  55.0 4.6 %collective-permute-start.8 = (bf16[4,576,128]{2,1,0:T(8,128)(2,1)S(1)}, bf16[4,576,128]{2,1,0:T(8,128)(2,1)S(1)}, u32[]{:S(2)}, u32[]{:S(2)}) collective-permute-start(bf16[4,576,128]{2,1,0:T(8,128)(2,1)S(1)} %shard_map.78.rest_5_), channel_id=1, source_target_pairs={{0,16},{16,0},{1,17},{17,1},{2,18},{18,2},{3,19},{19,3},{4,20},{20... | collective-permute-start | bytes 1769480 | tf_op jit(solution)/shard_map/ppermute | solution.py:38
  59.6 0.1 collective-permute-start.9
  59.7 1.5 %collective-permute-done.8.rest_8_ = bf16[4,576,128]{2,1,0:T(8,128)(2,1)S(1)} collective-permute-done((bf16[4,576,128]{2,1,0:T(8,128)(2,1)S(1)}, bf16[4,576,128]{2,1,0:T(8,128)(2,1)S(1)}, u32[]{:S(2)}, u32[]{:S(2)}) %collective-permute-start.8) | collective-permute-done | bytes 589856 | tf_op jit(solution)/shard_map/ppermute | solution.py:38
  61.2 0.8 %collective-permute-done.9.rest_9_ = bf16[4,576,128]{2,1,0:T(8,128)(2,1)S(1)} collective-permute-done((bf16[4,576,128]{2,1,0:T(8,128)(2,1)S(1)}, bf16[4,576,128]{2,1,0:T(8,128)(2,1)S(1)}, u32[]{:S(2)}, u32[]{:S(2)}) %collective-permute-start.9) | collective-permute-done | bytes 589856 | tf_op jit(solution)/shard_map/ppermute | solution.py:38
  62.0 10.0 %shard_map.80 = bf16[256,512]{1,0:T(8,128)(2,1)} custom-call(s32[3]{0:T(128)S(1)} %pad_add_fusion.place_ref, s32[16]{0:T(128)S(1)} %copy-done.4, bf16[2,576,512]{2,1,0:T(8,128)(2,1)S(1)} %shard_map.74.q_ref, bf16[4,512,128]{2,1,0:T(8,128)(2,1)S(1)} %copy-done.1, f32[2,512,512]{2,1,0:T(8,128)S(1)} %get-tuple-element.8.rest_1_, ...), custom_call_target="tpu_custom_call" | custom-call | flops 24000000 | bytes 24000 | tf_op jit(solution)/shard_map/pallas_call | solution.py:250
  (19 shorter events, 0.1 us)
Async XLA Ops:
  0.0 24.8 %copy-start.4 = (s32[16]{0:T(128)S(1)}, s32[16]{0:T(128)}, u32[]{:S(2)}) copy-start(s32[16]{0:T(128)} %owner_ref.3) | copy-start | bytes 196
  0.0 26.7 %copy-start.5 = (bf16[1536]{0:T(1024)(128)(2,1)S(1)}, bf16[1536]{0:T(1024)(128)(2,1)}, u32[]{:S(2)}) copy-start(bf16[1536]{0:T(1024)(128)(2,1)} %param.8) | copy-start | bytes 9220
  1.4 15.3 %all-to-all-start.1 = ((bf16[8,16,576]{2,1,0:T(8,128)(2,1)}), bf16[8,16,576]{2,1,0:T(8,128)(2,1)S(1)}, u32[]{:S(2)}, u32[]{:S(2)}) async-start(bf16[8,16,576]{2,1,0:T(8,128)(2,1)} %broadcast_in_dim.2), calls=%async_computation.1 | async-start | bytes 327680 | tf_op jit(solution)/shard_map/all_to_all | solution.py:277
  9.4 0.8 %copy-start.3 = (bf16[16,1536]{1,0:T(8,128)(2,1)S(1)}, bf16[16,1536]{1,0:T(8,128)(2,1)}, u32[]{:S(2)}) copy-start(bf16[16,1536]{1,0:T(8,128)(2,1)} %q_ref.1) | copy-start | bytes 147460
  16.7 29.0 %all-to-all-start = ((bf16[16,16,1536]{2,1,0:T(8,128)(2,1)}), bf16[16,16,1536]{2,1,0:T(8,128)(2,1)S(1)}, u32[]{:S(2)}, u32[]{:S(2)}) async-start(bf16[16,16,1536]{2,1,0:T(8,128)(2,1)} %shard_map.73), calls=%async_computation | async-start | bytes 1572864 | tf_op jit(solution)/shard_map/all_to_all | solution.py:282
  21.2 7.0 %collective-permute-start.2 = (bf16[128,576]{1,0:T(8,128)(2,1)S(1)}, bf16[128,576]{1,0:T(8,128)(2,1)S(1)}, u32[]{:S(2)}, u32[]{:S(2)}) collective-permute-start(bf16[128,576]{1,0:T(8,128)(2,1)S(1)} %bitcast.8), channel_id=1, source_target_pairs={{0,64},{16,144},{1,65},{17,145},{2,66},{18,146},{3,67},{19,147},{4... | collective-permute-start | bytes 442376 | tf_op jit(solution)/shard_map/ppermute | solution.py:38
  22.1 6.8 %collective-permute-start.1 = (bf16[128,576]{1,0:T(8,128)(2,1)S(1)}, bf16[128,576]{1,0:T(8,128)(2,1)S(1)}, u32[]{:S(2)}, u32[]{:S(2)}) collective-permute-start(bf16[128,576]{1,0:T(8,128)(2,1)S(1)} %bitcast.9), channel_id=1, source_target_pairs={{0,96},{16,152},{1,97},{17,153},{2,98},{18,154},{3,99},{19,155},{4... | collective-permute-start | bytes 442376 | tf_op jit(solution)/shard_map/ppermute | solution.py:38
  22.1 6.9 %collective-permute-start = (bf16[128,576]{1,0:T(8,128)(2,1)S(1)}, bf16[128,576]{1,0:T(8,128)(2,1)S(1)}, u32[]{:S(2)}, u32[]{:S(2)}) collective-permute-start(bf16[128,576]{1,0:T(8,128)(2,1)S(1)} %bitcast.10), channel_id=1, source_target_pairs={{0,32},{16,24},{1,33},{17,25},{2,34},{18,26},{3,35},{19,27},{4,36}... | collective-permute-start | bytes 442376 | tf_op jit(solution)/shard_map/ppermute | solution.py:38
  29.3 30.3 %collective-permute-start.6 = (bf16[4,576,128]{2,1,0:T(8,128)(2,1)S(1)}, bf16[4,576,128]{2,1,0:T(8,128)(2,1)S(1)}, u32[]{:S(2)}, u32[]{:S(2)}) collective-permute-start(bf16[4,576,128]{2,1,0:T(8,128)(2,1)S(1)} %shard_map.75.rest_0_), channel_id=1, source_target_pairs={{0,128},{16,80},{1,129},{17,81},{2,130},{18,82},{3,131},{19,83},{4... | collective-permute-start | bytes 1769480 | tf_op jit(solution)/shard_map/ppermute | solution.py:38
  32.1 22.8 %collective-permute-start.5 = (bf16[4,576,128]{2,1,0:T(8,128)(2,1)S(1)}, bf16[4,576,128]{2,1,0:T(8,128)(2,1)S(1)}, u32[]{:S(2)}, u32[]{:S(2)}) collective-permute-start(bf16[4,576,128]{2,1,0:T(8,128)(2,1)S(1)} %shard_map.75.rest_0_), channel_id=1, source_target_pairs={{0,136},{16,112},{1,137},{17,113},{2,138},{18,114},{3,139},{19,115... | collective-permute-start | bytes 1769480 | tf_op jit(solution)/shard_map/ppermute | solution.py:38
  33.0 21.9 %collective-permute-start.4 = (bf16[4,576,128]{2,1,0:T(8,128)(2,1)S(1)}, bf16[4,576,128]{2,1,0:T(8,128)(2,1)S(1)}, u32[]{:S(2)}, u32[]{:S(2)}) collective-permute-start(bf16[4,576,128]{2,1,0:T(8,128)(2,1)S(1)} %shard_map.75.rest_0_), channel_id=1, source_target_pairs={{0,8},{16,48},{1,9},{17,49},{2,10},{18,50},{3,11},{19,51},{4,12},{... | collective-permute-start | bytes 1769480 | tf_op jit(solution)/shard_map/ppermute | solution.py:38
  33.6 16.6 %collective-permute-start.3 = (bf16[4,576,128]{2,1,0:T(8,128)(2,1)S(1)}, bf16[4,576,128]{2,1,0:T(8,128)(2,1)}, u32[]{:S(2)}, u32[]{:S(2)}) collective-permute-start(bf16[4,576,128]{2,1,0:T(8,128)(2,1)S(1)} %shard_map.75.rest_0_), channel_id=1, source_target_pairs={{0,16},{16,0},{1,17},{17,1},{2,18},{18,2},{3,19},{19,3},{4,20},{20... | collective-permute-start | bytes 1769480 | tf_op jit(solution)/shard_map/ppermute | solution.py:38
  45.7 1.7 %copy-start = (bf16[1536,768]{1,0:T(8,128)(2,1)S(1)}, bf16[1536,768]{1,0:T(8,128)(2,1)}, u32[]{:S(2)}) copy-start(bf16[1536,768]{1,0:T(8,128)(2,1)} %up_ref.1) | copy-start | bytes 7077892
  47.4 1.0 %copy-start.2 = (bf16[4,128,512]{2,1,0:T(8,128)(2,1)S(1)}, bf16[4,128,512]{2,1,0:T(8,128)(2,1)}, u32[]{:S(2)}) copy-start(bf16[4,128,512]{2,1,0:T(8,128)(2,1)} %ak_ref.1) | copy-start | bytes 1572868
  54.8 7.2 %copy-start.1 = (bf16[4,512,128]{2,1,0:T(8,128)(2,1)S(1)}, bf16[4,512,128]{2,1,0:T(8,128)(2,1)}, u32[]{:S(2)}) copy-start(bf16[4,512,128]{2,1,0:T(8,128)(2,1)} %rest_0_.1) | copy-start | bytes 1572868
  54.9 4.8 %collective-permute-start.7 = (bf16[4,576,128]{2,1,0:T(8,128)(2,1)S(1)}, bf16[4,576,128]{2,1,0:T(8,128)(2,1)S(1)}, u32[]{:S(2)}, u32[]{:S(2)}) collective-permute-start(bf16[4,576,128]{2,1,0:T(8,128)(2,1)S(1)} %shard_map.77.rest_4_), channel_id=1, source_target_pairs={{0,16},{16,0},{1,17},{17,1},{2,18},{18,2},{3,19},{19,3},{4,20},{20... | collective-permute-start | bytes 1769480 | tf_op jit(solution)/shard_map/ppermute | solution.py:38
  55.0 6.2 %collective-permute-start.8 = (bf16[4,576,128]{2,1,0:T(8,128)(2,1)S(1)}, bf16[4,576,128]{2,1,0:T(8,128)(2,1)S(1)}, u32[]{:S(2)}, u32[]{:S(2)}) collective-permute-start(bf16[4,576,128]{2,1,0:T(8,128)(2,1)S(1)} %shard_map.78.rest_5_), channel_id=1, source_target_pairs={{0,16},{16,0},{1,17},{17,1},{2,18},{18,2},{3,19},{19,3},{4,20},{20... | collective-permute-start | bytes 1769480 | tf_op jit(solution)/shard_map/ppermute | solution.py:38
  59.6 2.5 %collective-permute-start.9 = (bf16[4,576,128]{2,1,0:T(8,128)(2,1)S(1)}, bf16[4,576,128]{2,1,0:T(8,128)(2,1)S(1)}, u32[]{:S(2)}, u32[]{:S(2)}) collective-permute-start(bf16[4,576,128]{2,1,0:T(8,128)(2,1)S(1)} %shard_map.79.rest_6_), channel_id=1, source_target_pairs={{0,16},{16,0},{1,17},{17,1},{2,18},{18,2},{3,19},{19,3},{4,20},{20... | collective-permute-start | bytes 1769480 | tf_op jit(solution)/shard_map/ppermute | solution.py:38

commit v4 on v3

--- a/solution.py
+++ b/solution.py
@@ -20,7 +20,7 @@
 SCALE2 = float(NOPE + ROPE) ** (-0.5) * math.log2(math.e)
 MASKED = -1e30
 AXES = ("ctx", "head")
-SHIFTS = (1, 3, 2)
+SHIFTS = (2, 3, 1)
 
 
 def flat(x, y, z, c):
@@ -45,12 +45,17 @@
     return to
 
 
+def swap_row(x, y, z, c):
+    return (x, y ^ 1, z, c)
+
+
 def swap_core(x, y, z, c):
     return (x, y, z, c + 1)
 
 
-def spread_kernel(q_ref, q_out):
-    q_out[...] = jnp.broadcast_to(q_ref[...][None], q_out.shape)
+def spread_kernel(q_ref, pair_ref, q_out):
+    both = jnp.concatenate([q_ref[...], pair_ref[...]], axis=0)
+    q_out[...] = jnp.broadcast_to(both[None], q_out.shape)
 
 
 def turn_kernel(*refs):
@@ -62,8 +67,11 @@
     pass
 
 
-def project_kernel(q_ref, gain_ref, cos_ref, sin_ref, up_ref, ak_ref, out_ref):
-    x = q_ref[...].astype(jnp.float32)
+def project_kernel(place_ref, q_ref, gain_ref, cos_ref, sin_ref, up_ref, ak_ref, out_ref):
+    own = place_ref[1] & 1
+    x = jnp.concatenate(
+        [q_ref[:, 16 * k : 16 * k + 16].reshape(HALF, QLAT) for k in range(2)], axis=0
+    ).astype(jnp.float32)
     ms = jnp.mean(x * x, axis=-1, keepdims=True)
     normed = (x * lax.rsqrt(ms + EPS) * gain_ref[...].astype(jnp.float32)).astype(jnp.bfloat16)
     proj = lax.dot_general(
@@ -79,10 +87,11 @@
         qa = lax.dot_general(
             ak_ref[h], nope, (((0,), (0,)), ((), ())), preferred_element_type=jnp.float32
         ).astype(jnp.bfloat16)
-        for half in range(2):
+        for k in range(2):
+            half = own if k == 0 else 1 - own
             cols = slice(h * HALF, (h + 1) * HALF)
-            out_ref[half, :LATENT, cols] = qa[:, half * HALF : (half + 1) * HALF]
-            out_ref[half, LATENT:, cols] = pe[:, half * HALF : (half + 1) * HALF]
+            out_ref[half, :LATENT, cols] = qa[:, k * HALF : (k + 1) * HALF]
+            out_ref[half, LATENT:, cols] = pe[:, k * HALF : (k + 1) * HALF]
 
 
 def attend_kernel(slots, first, last, place_ref, owner_ref, q_ref, *rest):
@@ -189,12 +198,16 @@
         s_now[...] = score(0)
 
     def step(t, _):
-        s_next[...] = score(jnp.minimum(t + 1, tiles - 1))
+        s_next[...] = score(t + 1)
         update(t, s_now[...])
         s_now[...] = s_next[...]
         return 0
 
-    lax.fori_loop(0, tiles, step, 0)
+    lax.fori_loop(0, tiles - 1, step, 0)
+
+    @pl.when(tiles > 0)
+    def _():
+        update(tiles - 1, s_now[...])
 
     if last:
         av_copy.wait()
@@ -266,20 +279,21 @@
     me_x, me_y, me_c = (ctx // 2) % 4, (ctx // 8) * 2 + head // 8, ctx % 2
     place = jnp.stack([me_x, me_y, me_c]).astype(jnp.int32)
 
+    z_groups = [list(range(8)), list(range(8, 16))]
     q_spread = pl.pallas_call(
         spread_kernel,
-        out_shape=jax.ShapeDtypeStruct((16,) + query_latent.shape, jnp.bfloat16),
-        in_specs=[VM],
+        out_shape=jax.ShapeDtypeStruct((8, 32, QLAT), jnp.bfloat16),
+        in_specs=[VM] * 2,
         out_specs=VM,
         compiler_params=pltpu.CompilerParams(vmem_limit_bytes=4 * 2**20),
-    )(query_latent)
+    )(query_latent, move(query_latent, swap_row))
 
     own = lax.all_to_all(
         jnp.broadcast_to(kv_latent[None], (8,) + kv_latent.shape),
-        "head", 0, 0, axis_index_groups=[list(range(8)), list(range(8, 16))], tiled=True
+        "head", 0, 0, axis_index_groups=z_groups, tiled=True
     ).reshape(HALF, KV)
 
-    rows = lax.all_to_all(q_spread, "head", 0, 0, tiled=True).reshape(256, QLAT)
+    rows = lax.all_to_all(q_spread, "head", 0, 0, axis_index_groups=z_groups, tiled=True)
 
     blocks = [own] + [move(own, shift(k, True)) for k in SHIFTS]
     stack = pl.pallas_call(
@@ -294,17 +308,18 @@
         near[k] = move(stack, shift(k, False))
     p = block_owner[ctx]
     offset = jnp.arange(256, dtype=jnp.int32)
-    pos = jnp.where(offset < HALF, p * HALF + offset, (NB - 1 - p) * HALF + offset - HALF)
+    in_low = (offset < HALF) == (me_y % 2 == 0)
+    pos = jnp.where(in_low, p, NB - 1 - p) * HALF + (offset & (HALF - 1))
     freq = jnp.exp(jnp.arange(ROPE // 2, dtype=jnp.float32) * (-math.log(10000.0) / (ROPE // 2)))
     angles = freq[:, None] * pos.astype(jnp.float32)
     queries = pl.pallas_call(
         project_kernel,
         out_shape=jax.ShapeDtypeStruct((2, KV, 512), jnp.bfloat16),
-        in_specs=[VM] * 6,
+        in_specs=[SM] + [VM] * 6,
         out_specs=VM,
         compiler_params=pltpu.CompilerParams(vmem_limit_bytes=16 * 2**20),
         cost_estimate=pl.CostEstimate(flops=750_000_000, bytes_accessed=5_000_000, transcendentals=0),
-    )(rows, norm_gain.reshape(1, QLAT), jnp.cos(angles), jnp.sin(angles), q_up, absorb_key)
+    )(place, rows, norm_gain.reshape(1, QLAT), jnp.cos(angles), jnp.sin(angles), q_up, absorb_key)
 
     distant = {0: move(stack, swap_core)}
 

time: 72.3 us -> 68.5 us (0.947)
  the two profiles are of different devices: /device:TPU:57 before, /device:TPU:1 now
where the time goes in v4:
time: 68.5 us; the launch traced here: 68 us
  starting transfers between devices  31.3 us (46%)
  Pallas kernels  16.6 us (24%)
  waiting for transfers between devices  12.8 us (19%)
  local copies, waits for them, and re-layouts  5.58 us (8%)
  other arithmetic  0.9 us (1%)
  between operations  0.74 us (1%)
    ppermute x11, starting transfers between devices, move(): return lax.ppermute(a, AXES, pairs)  18.6 us
    pallas_call x2, Pallas kernels, attend(): pl.pallas_call(functools.partial(attend_kernel, slots, first, last), out_...  13.1 us
    all_to_all x1, starting transfers between devices, per_device(): lax.all_to_all(jnp.broadcast_to(kv_latent[None], (8,) + kv_latent.shape),...  9.01 us
    ppermute x11, waiting for transfers between devices, move(): return lax.ppermute(a, AXES, pairs)  7.49 us
    all_to_all x1, starting transfers between devices, per_device(): lax.all_to_all(q_spread, 'head', 0, 0, axis_index_groups=z_groups, tiled=...  3.69 us
    unnamed x12, local copies, waits for them, and re-layouts  3.52 us
    all_to_all x1, waiting for transfers between devices, per_device(): lax.all_to_all(jnp.broadcast_to(kv_latent[None], (8,) + kv_latent.shape),...  3.26 us
    pallas_call x1, Pallas kernels, per_device(): pl.pallas_call(project_kernel, out_shape=jax.ShapeDtypeStruct((2, KV, 512...  2.32 us
  transfers between devices with their start and end apart: 13, of which 7 were waited for; matrix products, arithmetic and copies ran while one was open for 2% of the time, Pallas kernels for 11%

profile of v4, /device:TPU:1, one launch (start us, length us, event | category | flops | bytes accessed | tf_op | source)
XLA Modules:
  0.0 68.0 jit_solution(1593446627770539852)
XLA Ops:
  0.0 1.4 %broadcast_in_dim.18 = bf16[8,16,576]{2,1,0:T(8,128)(2,1)} broadcast(bf16[16,576]{1,0:T(8,128)(2,1)} %param.9), dimensions={1,2} | broadcast | bytes 165888 | tf_op jit(solution)/shard_map/broadcast_in_dim | solution.py:292
  1.4 9.0 %all-to-all-start.1 = ((bf16[8,16,576]{2,1,0:T(8,128)(2,1)}), bf16[8,16,576]{2,1,0:T(8,128)(2,1)S(1)}, u32[]{:S(2)}, u32[]{:S(2)}) async-start(bf16[8,16,576]{2,1,0:T(8,128)(2,1)} %broadcast_in_dim.18), calls=%async_computation.1 | async-start | bytes 327680 | tf_op jit(solution)/shard_map/all_to_all | solution.py:291
  10.5 1.3 %collective-permute-start = (bf16[16,1536]{1,0:T(8,128)(2,1)}, bf16[16,1536]{1,0:T(8,128)(2,1)S(1)}, u32[]{:S(2)}, u32[]{:S(2)}) collective-permute-start(bf16[16,1536]{1,0:T(8,128)(2,1)} %q_ref.1), channel_id=1, source_target_pairs={{0,8},{16,24},{1,9},{17,25},{2,10},{18,26},{3,11},{19,27},{4,12},{... | collective-permute-start | bytes 147464 | tf_op jit(solution)/shard_map/ppermute | solution.py:38
  11.7 1.9 %collective-permute-done.pair_ref = bf16[16,1536]{1,0:T(8,128)(2,1)S(1)} collective-permute-done((bf16[16,1536]{1,0:T(8,128)(2,1)}, bf16[16,1536]{1,0:T(8,128)(2,1)S(1)}, u32[]{:S(2)}, u32[]{:S(2)}) %collective-permute-start) | collective-permute-done | bytes 49184 | tf_op jit(solution)/shard_map/ppermute | solution.py:38
  13.6 0.8 %copy-done.3 = bf16[16,1536]{1,0:T(8,128)(2,1)S(1)} copy-done((bf16[16,1536]{1,0:T(8,128)(2,1)S(1)}, bf16[16,1536]{1,0:T(8,128)(2,1)}, u32[]{:S(2)}) %copy-start.3) | copy-done | bytes 49176
  14.4 0.9 %shard_map.73 = bf16[8,32,1536]{2,1,0:T(8,128)(2,1)} custom-call(bf16[16,1536]{1,0:T(8,128)(2,1)S(1)} %copy-done.3, bf16[16,1536]{1,0:T(8,128)(2,1)S(1)} %collective-permute-done.pair_ref), custom_call_target="tpu_custom_call" | custom-call | tf_op jit(solution)/shard_map/pallas_call | solution.py:283
  15.3 3.3 %all-to-all-done.1 = bf16[8,16,576]{2,1,0:T(8,128)(2,1)S(1)} async-done(((bf16[8,16,576]{2,1,0:T(8,128)(2,1)}), bf16[8,16,576]{2,1,0:T(8,128)(2,1)S(1)}, u32[]{:S(2)}, u32[]{:S(2)}) %all-to-all-start.1) | async-done | bytes 147488 | tf_op jit(solution)/shard_map/all_to_all | solution.py:291
  18.6 3.7 %all-to-all-start = ((bf16[8,32,1536]{2,1,0:T(8,128)(2,1)}), bf16[8,32,1536]{2,1,0:T(8,128)(2,1)S(1)}, u32[]{:S(2)}, u32[]{:S(2)}) async-start(bf16[8,32,1536]{2,1,0:T(8,128)(2,1)} %shard_map.73), calls=%async_computation | async-start | bytes 1572864 | tf_op jit(solution)/shard_map/all_to_all | solution.py:296
  22.3 1.3 %collective-permute-start.3 = (bf16[128,576]{1,0:T(8,128)(2,1)S(1)}, bf16[128,576]{1,0:T(8,128)(2,1)S(1)}, u32[]{:S(2)}, u32[]{:S(2)}) collective-permute-start(bf16[128,576]{1,0:T(8,128)(2,1)S(1)} %bitcast.5), channel_id=1, source_target_pairs={{0,32},{16,24},{1,33},{17,25},{2,34},{18,26},{3,35},{19,27},{4,36}... | collective-permute-start | bytes 442376 | tf_op jit(solution)/shard_map/ppermute | solution.py:38
  23.6 1.5 %collective-permute-start.2 = (bf16[128,576]{1,0:T(8,128)(2,1)S(1)}, bf16[128,576]{1,0:T(8,128)(2,1)S(1)}, u32[]{:S(2)}, u32[]{:S(2)}) collective-permute-start(bf16[128,576]{1,0:T(8,128)(2,1)S(1)} %bitcast.6), channel_id=1, source_target_pairs={{0,96},{16,152},{1,97},{17,153},{2,98},{18,154},{3,99},{19,155},{4... | collective-permute-start | bytes 442376 | tf_op jit(solution)/shard_map/ppermute | solution.py:38
  25.1 1.6 %collective-permute-start.1 = (bf16[128,576]{1,0:T(8,128)(2,1)S(1)}, bf16[128,576]{1,0:T(8,128)(2,1)S(1)}, u32[]{:S(2)}, u32[]{:S(2)}) collective-permute-start(bf16[128,576]{1,0:T(8,128)(2,1)S(1)} %bitcast.7), channel_id=1, source_target_pairs={{0,64},{16,144},{1,65},{17,145},{2,66},{18,146},{3,67},{19,147},{4... | collective-permute-start | bytes 442376 | tf_op jit(solution)/shard_map/ppermute | solution.py:38
  26.7 0.6 dynamic_slice.3
  28.0 2.8 %collective-permute-done.1.refs_1_ = bf16[128,576]{1,0:T(8,128)(2,1)S(1)} collective-permute-done((bf16[128,576]{1,0:T(8,128)(2,1)S(1)}, bf16[128,576]{1,0:T(8,128)(2,1)S(1)}, u32[]{:S(2)}, u32[]{:S(2)}) %collective-permute-start.1) | collective-permute-done | bytes 147488 | tf_op jit(solution)/shard_map/ppermute | solution.py:38
  30.8 0.2 shard_map.75.rest_0_
  31.0 2.8 %collective-permute-start.7 = (bf16[4,576,128]{2,1,0:T(8,128)(2,1)S(1)}, bf16[4,576,128]{2,1,0:T(8,128)(2,1)S(1)}, u32[]{:S(2)}, u32[]{:S(2)}) collective-permute-start(bf16[4,576,128]{2,1,0:T(8,128)(2,1)S(1)} %shard_map.75.rest_0_), channel_id=1, source_target_pairs={{0,128},{16,80},{1,129},{17,81},{2,130},{18,82},{3,131},{19,83},{4... | collective-permute-start | bytes 1769480 | tf_op jit(solution)/shard_map/ppermute | solution.py:38
  33.9 0.9 %collective-permute-start.6 = (bf16[4,576,128]{2,1,0:T(8,128)(2,1)S(1)}, bf16[4,576,128]{2,1,0:T(8,128)(2,1)S(1)}, u32[]{:S(2)}, u32[]{:S(2)}) collective-permute-start(bf16[4,576,128]{2,1,0:T(8,128)(2,1)S(1)} %shard_map.75.rest_0_), channel_id=1, source_target_pairs={{0,136},{16,112},{1,137},{17,113},{2,138},{18,114},{3,139},{19,115... | collective-permute-start | bytes 1769480 | tf_op jit(solution)/shard_map/ppermute | solution.py:38
  34.7 0.6 collective-permute-start.5
  35.3 5.2 %collective-permute-start.4 = (bf16[4,576,128]{2,1,0:T(8,128)(2,1)S(1)}, bf16[4,576,128]{2,1,0:T(8,128)(2,1)}, u32[]{:S(2)}, u32[]{:S(2)}) collective-permute-start(bf16[4,576,128]{2,1,0:T(8,128)(2,1)S(1)} %shard_map.75.rest_0_), channel_id=1, source_target_pairs={{0,16},{16,0},{1,17},{17,1},{2,18},{18,2},{3,19},{19,3},{4,20},{20... | collective-permute-start | bytes 1769480 | tf_op jit(solution)/shard_map/ppermute | solution.py:38
  40.6 0.6 fusion.2
  41.3 0.2 multiply_sine_fusion
  41.5 2.1 %all-to-all-done.q_ref = bf16[8,32,1536]{2,1,0:T(8,128)(2,1)S(1)} async-done(((bf16[8,32,1536]{2,1,0:T(8,128)(2,1)}), bf16[8,32,1536]{2,1,0:T(8,128)(2,1)S(1)}, u32[]{:S(2)}, u32[]{:S(2)}) %all-to-all-start) | async-done | bytes 786464 | tf_op jit(solution)/shard_map/all_to_all | solution.py:296
  43.6 1.7 %copy-done = bf16[1536,768]{1,0:T(8,128)(2,1)S(1)} copy-done((bf16[1536,768]{1,0:T(8,128)(2,1)S(1)}, bf16[1536,768]{1,0:T(8,128)(2,1)}, u32[]{:S(2)}) %copy-start) | copy-done | bytes 2359320
  45.2 1.0 %copy-done.2 = bf16[4,128,512]{2,1,0:T(8,128)(2,1)S(1)} copy-done((bf16[4,128,512]{2,1,0:T(8,128)(2,1)S(1)}, bf16[4,128,512]{2,1,0:T(8,128)(2,1)}, u32[]{:S(2)}) %copy-start.2) | copy-done | bytes 524312
  46.3 2.3 %shard_map.74.q_ref = bf16[2,576,512]{2,1,0:T(8,128)(2,1)S(1)} custom-call(s32[3]{0:T(128)S(1)} %pad_add_fusion.place_ref, bf16[8,32,1536]{2,1,0:T(8,128)(2,1)S(1)} %all-to-all-done.q_ref, bf16[1,1536]{1,0:T(2,128)(2,1)S(1)} %reshape.23.gain_ref, f32[32,256]{1,0:T(8,128)S(1)} %get-tuple-element.12.cos_ref, f32[32,256]{1,0:T(8,128)S(1)} %get-tuple-element.11.sin_ref, ...), custom_call_target="tpu_custom_call" | custom-call | flops 750000000 | bytes 5000000 | tf_op jit(solution)/shard_map/pallas_call | solution.py:315
  48.6 4.3 %shard_map.76 = (f32[2,512,512]{2,1,0:T(8,128)S(1)}, f32[2,1,512]{2,1,0:T(1,128)S(1)}, f32[2,1,512]{2,1,0:T(1,128)S(1)}) custom-call(s32[3]{0:T(128)S(1)} %pad_add_fusion.place_ref, s32[16]{0:T(128)S(1)} %copy-done.4, bf16[2,576,512]{2,1,0:T(8,128)(2,1)S(1)} %shard_map.74.q_ref, bf16[4,576,128]{2,1,0:T(8,128)(2,1)S(1)} %shard_map.75.rest_0_, ...), custom_call_target="tpu_custom_call" | custom-call | flops 8000000 | bytes 8000 | tf_op jit(solution)/shard_map/pallas_call | solution.py:263
  52.9 2.9 %collective-permute-start.8 = (bf16[4,576,128]{2,1,0:T(8,128)(2,1)S(1)}, bf16[4,576,128]{2,1,0:T(8,128)(2,1)S(1)}, u32[]{:S(2)}, u32[]{:S(2)}) collective-permute-start(bf16[4,576,128]{2,1,0:T(8,128)(2,1)S(1)} %shard_map.77.rest_4_), channel_id=1, source_target_pairs={{0,16},{16,0},{1,17},{17,1},{2,18},{18,2},{3,19},{19,3},{4,20},{20... | collective-permute-start | bytes 1769480 | tf_op jit(solution)/shard_map/ppermute | solution.py:38
  55.8 0.1 collective-permute-start.9
  56.0 0.4 collective-permute-start.10
  56.4 1.1 %collective-permute-done.8.rest_7_ = bf16[4,576,128]{2,1,0:T(8,128)(2,1)S(1)} collective-permute-done((bf16[4,576,128]{2,1,0:T(8,128)(2,1)S(1)}, bf16[4,576,128]{2,1,0:T(8,128)(2,1)S(1)}, u32[]{:S(2)}, u32[]{:S(2)}) %collective-permute-start.8) | collective-permute-done | bytes 589856 | tf_op jit(solution)/shard_map/ppermute | solution.py:38
  57.5 0.8 %collective-permute-done.9.rest_8_ = bf16[4,576,128]{2,1,0:T(8,128)(2,1)S(1)} collective-permute-done((bf16[4,576,128]{2,1,0:T(8,128)(2,1)S(1)}, bf16[4,576,128]{2,1,0:T(8,128)(2,1)S(1)}, u32[]{:S(2)}, u32[]{:S(2)}) %collective-permute-start.9) | collective-permute-done | bytes 589856 | tf_op jit(solution)/shard_map/ppermute | solution.py:38
  58.3 0.8 %collective-permute-done.10.rest_9_ = bf16[4,576,128]{2,1,0:T(8,128)(2,1)S(1)} collective-permute-done((bf16[4,576,128]{2,1,0:T(8,128)(2,1)S(1)}, bf16[4,576,128]{2,1,0:T(8,128)(2,1)S(1)}, u32[]{:S(2)}, u32[]{:S(2)}) %collective-permute-start.10) | collective-permute-done | bytes 589856 | tf_op jit(solution)/shard_map/ppermute | solution.py:38
  59.2 8.8 %shard_map.80 = bf16[256,512]{1,0:T(8,128)(2,1)} custom-call(s32[3]{0:T(128)S(1)} %pad_add_fusion.place_ref, s32[16]{0:T(128)S(1)} %copy-done.4, bf16[2,576,512]{2,1,0:T(8,128)(2,1)S(1)} %shard_map.74.q_ref, bf16[4,512,128]{2,1,0:T(8,128)(2,1)S(1)} %copy-done.1, f32[2,512,512]{2,1,0:T(8,128)S(1)} %get-tuple-element.8.rest_1_, ...), custom_call_target="tpu_custom_call" | custom-call | flops 24000000 | bytes 24000 | tf_op jit(solution)/shard_map/pallas_call | solution.py:263
  (21 shorter events, 0.1 us)
Async XLA Ops:
  0.0 26.7 %copy-start.5 = (bf16[1536]{0:T(1024)(128)(2,1)S(1)}, bf16[1536]{0:T(1024)(128)(2,1)}, u32[]{:S(2)}) copy-start(bf16[1536]{0:T(1024)(128)(2,1)} %param.8) | copy-start | bytes 9220
  0.0 26.7 %copy-start.4 = (s32[16]{0:T(128)S(1)}, s32[16]{0:T(128)}, u32[]{:S(2)}) copy-start(s32[16]{0:T(128)} %owner_ref.3) | copy-start | bytes 196
  1.4 17.2 %all-to-all-start.1 = ((bf16[8,16,576]{2,1,0:T(8,128)(2,1)}), bf16[8,16,576]{2,1,0:T(8,128)(2,1)S(1)}, u32[]{:S(2)}, u32[]{:S(2)}) async-start(bf16[8,16,576]{2,1,0:T(8,128)(2,1)} %broadcast_in_dim.18), calls=%async_computation.1 | async-start | bytes 327680 | tf_op jit(solution)/shard_map/all_to_all | solution.py:291
  10.5 3.2 %collective-permute-start = (bf16[16,1536]{1,0:T(8,128)(2,1)}, bf16[16,1536]{1,0:T(8,128)(2,1)S(1)}, u32[]{:S(2)}, u32[]{:S(2)}) collective-permute-start(bf16[16,1536]{1,0:T(8,128)(2,1)} %q_ref.1), channel_id=1, source_target_pairs={{0,8},{16,24},{1,9},{17,25},{2,10},{18,26},{3,11},{19,27},{4,12},{... | collective-permute-start | bytes 147464 | tf_op jit(solution)/shard_map/ppermute | solution.py:38
  13.6 0.8 %copy-start.3 = (bf16[16,1536]{1,0:T(8,128)(2,1)S(1)}, bf16[16,1536]{1,0:T(8,128)(2,1)}, u32[]{:S(2)}) copy-start(bf16[16,1536]{1,0:T(8,128)(2,1)} %q_ref.1) | copy-start | bytes 147460
  18.6 25.0 %all-to-all-start = ((bf16[8,32,1536]{2,1,0:T(8,128)(2,1)}), bf16[8,32,1536]{2,1,0:T(8,128)(2,1)S(1)}, u32[]{:S(2)}, u32[]{:S(2)}) async-start(bf16[8,32,1536]{2,1,0:T(8,128)(2,1)} %shard_map.73), calls=%async_computation | async-start | bytes 1572864 | tf_op jit(solution)/shard_map/all_to_all | solution.py:296
  22.3 5.7 %collective-permute-start.3 = (bf16[128,576]{1,0:T(8,128)(2,1)S(1)}, bf16[128,576]{1,0:T(8,128)(2,1)S(1)}, u32[]{:S(2)}, u32[]{:S(2)}) collective-permute-start(bf16[128,576]{1,0:T(8,128)(2,1)S(1)} %bitcast.5), channel_id=1, source_target_pairs={{0,32},{16,24},{1,33},{17,25},{2,34},{18,26},{3,35},{19,27},{4,36}... | collective-permute-start | bytes 442376 | tf_op jit(solution)/shard_map/ppermute | solution.py:38
  23.6 4.4 %collective-permute-start.2 = (bf16[128,576]{1,0:T(8,128)(2,1)S(1)}, bf16[128,576]{1,0:T(8,128)(2,1)S(1)}, u32[]{:S(2)}, u32[]{:S(2)}) collective-permute-start(bf16[128,576]{1,0:T(8,128)(2,1)S(1)} %bitcast.6), channel_id=1, source_target_pairs={{0,96},{16,152},{1,97},{17,153},{2,98},{18,154},{3,99},{19,155},{4... | collective-permute-start | bytes 442376 | tf_op jit(solution)/shard_map/ppermute | solution.py:38
  25.1 5.7 %collective-permute-start.1 = (bf16[128,576]{1,0:T(8,128)(2,1)S(1)}, bf16[128,576]{1,0:T(8,128)(2,1)S(1)}, u32[]{:S(2)}, u32[]{:S(2)}) collective-permute-start(bf16[128,576]{1,0:T(8,128)(2,1)S(1)} %bitcast.7), channel_id=1, source_target_pairs={{0,64},{16,144},{1,65},{17,145},{2,66},{18,146},{3,67},{19,147},{4... | collective-permute-start | bytes 442376 | tf_op jit(solution)/shard_map/ppermute | solution.py:38
  31.0 24.9 %collective-permute-start.7 = (bf16[4,576,128]{2,1,0:T(8,128)(2,1)S(1)}, bf16[4,576,128]{2,1,0:T(8,128)(2,1)S(1)}, u32[]{:S(2)}, u32[]{:S(2)}) collective-permute-start(bf16[4,576,128]{2,1,0:T(8,128)(2,1)S(1)} %shard_map.75.rest_0_), channel_id=1, source_target_pairs={{0,128},{16,80},{1,129},{17,81},{2,130},{18,82},{3,131},{19,83},{4... | collective-permute-start | bytes 1769480 | tf_op jit(solution)/shard_map/ppermute | solution.py:38
  33.9 22.0 %collective-permute-start.6 = (bf16[4,576,128]{2,1,0:T(8,128)(2,1)S(1)}, bf16[4,576,128]{2,1,0:T(8,128)(2,1)S(1)}, u32[]{:S(2)}, u32[]{:S(2)}) collective-permute-start(bf16[4,576,128]{2,1,0:T(8,128)(2,1)S(1)} %shard_map.75.rest_0_), channel_id=1, source_target_pairs={{0,136},{16,112},{1,137},{17,113},{2,138},{18,114},{3,139},{19,115... | collective-permute-start | bytes 1769480 | tf_op jit(solution)/shard_map/ppermute | solution.py:38
  34.7 18.2 %collective-permute-start.5 = (bf16[4,576,128]{2,1,0:T(8,128)(2,1)S(1)}, bf16[4,576,128]{2,1,0:T(8,128)(2,1)S(1)}, u32[]{:S(2)}, u32[]{:S(2)}) collective-permute-start(bf16[4,576,128]{2,1,0:T(8,128)(2,1)S(1)} %shard_map.75.rest_0_), channel_id=1, source_target_pairs={{0,8},{16,48},{1,9},{17,49},{2,10},{18,50},{3,11},{19,51},{4,12},{... | collective-permute-start | bytes 1769480 | tf_op jit(solution)/shard_map/ppermute | solution.py:38
  35.3 13.3 %collective-permute-start.4 = (bf16[4,576,128]{2,1,0:T(8,128)(2,1)S(1)}, bf16[4,576,128]{2,1,0:T(8,128)(2,1)}, u32[]{:S(2)}, u32[]{:S(2)}) collective-permute-start(bf16[4,576,128]{2,1,0:T(8,128)(2,1)S(1)} %shard_map.75.rest_0_), channel_id=1, source_target_pairs={{0,16},{16,0},{1,17},{17,1},{2,18},{18,2},{3,19},{19,3},{4,20},{20... | collective-permute-start | bytes 1769480 | tf_op jit(solution)/shard_map/ppermute | solution.py:38
  43.6 1.7 %copy-start = (bf16[1536,768]{1,0:T(8,128)(2,1)S(1)}, bf16[1536,768]{1,0:T(8,128)(2,1)}, u32[]{:S(2)}) copy-start(bf16[1536,768]{1,0:T(8,128)(2,1)} %up_ref.1) | copy-start | bytes 7077892
  45.2 1.0 %copy-start.2 = (bf16[4,128,512]{2,1,0:T(8,128)(2,1)S(1)}, bf16[4,128,512]{2,1,0:T(8,128)(2,1)}, u32[]{:S(2)}) copy-start(bf16[4,128,512]{2,1,0:T(8,128)(2,1)} %ak_ref.1) | copy-start | bytes 1572868
  52.9 6.2 %copy-start.1 = (bf16[4,512,128]{2,1,0:T(8,128)(2,1)S(1)}, bf16[4,512,128]{2,1,0:T(8,128)(2,1)}, u32[]{:S(2)}) copy-start(bf16[4,512,128]{2,1,0:T(8,128)(2,1)} %rest_0_.1) | copy-start | bytes 1572868
  52.9 4.5 %collective-permute-start.8 = (bf16[4,576,128]{2,1,0:T(8,128)(2,1)S(1)}, bf16[4,576,128]{2,1,0:T(8,128)(2,1)S(1)}, u32[]{:S(2)}, u32[]{:S(2)}) collective-permute-start(bf16[4,576,128]{2,1,0:T(8,128)(2,1)S(1)} %shard_map.77.rest_4_), channel_id=1, source_target_pairs={{0,16},{16,0},{1,17},{17,1},{2,18},{18,2},{3,19},{19,3},{4,20},{20... | collective-permute-start | bytes 1769480 | tf_op jit(solution)/shard_map/ppermute | solution.py:38
  55.8 2.5 %collective-permute-start.9 = (bf16[4,576,128]{2,1,0:T(8,128)(2,1)S(1)}, bf16[4,576,128]{2,1,0:T(8,128)(2,1)S(1)}, u32[]{:S(2)}, u32[]{:S(2)}) collective-permute-start(bf16[4,576,128]{2,1,0:T(8,128)(2,1)S(1)} %shard_map.78.rest_5_), channel_id=1, source_target_pairs={{0,16},{16,0},{1,17},{17,1},{2,18},{18,2},{3,19},{19,3},{4,20},{20... | collective-permute-start | bytes 1769480 | tf_op jit(solution)/shard_map/ppermute | solution.py:38
  56.0 3.2 %collective-permute-start.10 = (bf16[4,576,128]{2,1,0:T(8,128)(2,1)S(1)}, bf16[4,576,128]{2,1,0:T(8,128)(2,1)S(1)}, u32[]{:S(2)}, u32[]{:S(2)}) collective-permute-start(bf16[4,576,128]{2,1,0:T(8,128)(2,1)S(1)} %shard_map.79.rest_6_), channel_id=1, source_target_pairs={{0,16},{16,0},{1,17},{17,1},{2,18},{18,2},{3,19},{19,3},{4,20},{20... | collective-permute-start | bytes 1769480 | tf_op jit(solution)/shard_map/ppermute | solution.py:38

commit v5 on v4

--- a/solution.py
+++ b/solution.py
@@ -69,11 +69,13 @@
 
 def project_kernel(place_ref, q_ref, gain_ref, cos_ref, sin_ref, up_ref, ak_ref, out_ref):
     own = place_ref[1] & 1
-    x = jnp.concatenate(
-        [q_ref[:, 16 * k : 16 * k + 16].reshape(HALF, QLAT) for k in range(2)], axis=0
-    ).astype(jnp.float32)
-    ms = jnp.mean(x * x, axis=-1, keepdims=True)
-    normed = (x * lax.rsqrt(ms + EPS) * gain_ref[...].astype(jnp.float32)).astype(jnp.bfloat16)
+    gain = gain_ref[...].astype(jnp.float32)
+    halves = []
+    for k in range(2):
+        x = q_ref[:, 16 * k : 16 * k + 16].reshape(HALF, QLAT).astype(jnp.float32)
+        ms = jnp.mean(x * x, axis=-1, keepdims=True)
+        halves.append((x * lax.rsqrt(ms + EPS) * gain).astype(jnp.bfloat16))
+    normed = jnp.concatenate(halves, axis=0)
     proj = lax.dot_general(
         up_ref[...], normed, (((0,), (1,)), ((), ())), preferred_element_type=jnp.float32
     )
@@ -214,7 +216,7 @@
         for half in range(2):
             for h in range(HD):
                 cols = slice(h * HALF, (h + 1) * HALF)
-                lat = (acc[half, :, cols] / l_ref[half, :, cols]).astype(jnp.bfloat16)
+                lat = (acc[half, :, cols] * (1.0 / l_ref[half, :, cols])).astype(jnp.bfloat16)
                 out_ref[half * HALF : (half + 1) * HALF, cols] = lax.dot_general(
                     lat, av_ref[h], (((0,), (0,)), ((), ())), preferred_element_type=jnp.float32
                 ).astype(jnp.bfloat16)

time: 68.5 us -> 69.1 us (level)
  the two profiles are of different devices: /device:TPU:1 before, /device:TPU:29 now
where the time goes in v5:
time: 69.1 us; the launch traced here: 68.2 us
  starting transfers between devices  27.7 us (40%)
  Pallas kernels  16.6 us (24%)
  waiting for transfers between devices  16.5 us (24%)
  local copies, waits for them, and re-layouts  5.58 us (8%)
  other arithmetic  0.9 us (1%)
  between operations  0.89 us (1%)
    ppermute x11, starting transfers between devices, move(): return lax.ppermute(a, AXES, pairs)  15.9 us
    pallas_call x2, Pallas kernels, attend(): pl.pallas_call(functools.partial(attend_kernel, slots, first, last), out_...  13.1 us
    ppermute x11, waiting for transfers between devices, move(): return lax.ppermute(a, AXES, pairs)  9.02 us
    all_to_all x1, starting transfers between devices, per_device(): lax.all_to_all(jnp.broadcast_to(kv_latent[None], (8,) + kv_latent.shape),...  8.19 us
    all_to_all x1, waiting for transfers between devices, per_device(): lax.all_to_all(q_spread, 'head', 0, 0, axis_index_groups=z_groups, tiled=...  4.22 us
    all_to_all x1, starting transfers between devices, per_device(): lax.all_to_all(q_spread, 'head', 0, 0, axis_index_groups=z_groups, tiled=...  3.69 us
    unnamed x12, local copies, waits for them, and re-layouts  3.52 us
    all_to_all x1, waiting for transfers between devices, per_device(): lax.all_to_all(jnp.broadcast_to(kv_latent[None], (8,) + kv_latent.shape),...  3.26 us
  transfers between devices with their start and end apart: 13, of which 9 were waited for; matrix products, arithmetic and copies ran while one was open for 2% of the time, Pallas kernels for 10%

profile of v5, /device:TPU:29, one launch (start us, length us, event | category | flops | bytes accessed | tf_op | source)
XLA Modules:
  0.0 68.2 jit_solution(5390715665890852699)
XLA Ops:
  0.0 1.4 %broadcast_in_dim.18 = bf16[8,16,576]{2,1,0:T(8,128)(2,1)} broadcast(bf16[16,576]{1,0:T(8,128)(2,1)} %param.9), dimensions={1,2} | broadcast | bytes 165888 | tf_op jit(solution)/shard_map/broadcast_in_dim | solution.py:294
  1.4 8.2 %all-to-all-start.1 = ((bf16[8,16,576]{2,1,0:T(8,128)(2,1)}), bf16[8,16,576]{2,1,0:T(8,128)(2,1)S(1)}, u32[]{:S(2)}, u32[]{:S(2)}) async-start(bf16[8,16,576]{2,1,0:T(8,128)(2,1)} %broadcast_in_dim.18), calls=%async_computation.1 | async-start | bytes 327680 | tf_op jit(solution)/shard_map/all_to_all | solution.py:293
  9.6 0.5 collective-permute-start
  10.1 2.7 %collective-permute-done.pair_ref = bf16[16,1536]{1,0:T(8,128)(2,1)S(1)} collective-permute-done((bf16[16,1536]{1,0:T(8,128)(2,1)}, bf16[16,1536]{1,0:T(8,128)(2,1)S(1)}, u32[]{:S(2)}, u32[]{:S(2)}) %collective-permute-start) | collective-permute-done | bytes 49184 | tf_op jit(solution)/shard_map/ppermute | solution.py:38
  12.8 0.8 %copy-done.3 = bf16[16,1536]{1,0:T(8,128)(2,1)S(1)} copy-done((bf16[16,1536]{1,0:T(8,128)(2,1)S(1)}, bf16[16,1536]{1,0:T(8,128)(2,1)}, u32[]{:S(2)}) %copy-start.3) | copy-done | bytes 49176
  13.6 0.9 %shard_map.73 = bf16[8,32,1536]{2,1,0:T(8,128)(2,1)} custom-call(bf16[16,1536]{1,0:T(8,128)(2,1)S(1)} %copy-done.3, bf16[16,1536]{1,0:T(8,128)(2,1)S(1)} %collective-permute-done.pair_ref), custom_call_target="tpu_custom_call" | custom-call | tf_op jit(solution)/shard_map/pallas_call | solution.py:285
  14.5 3.3 %all-to-all-done.1 = bf16[8,16,576]{2,1,0:T(8,128)(2,1)S(1)} async-done(((bf16[8,16,576]{2,1,0:T(8,128)(2,1)}), bf16[8,16,576]{2,1,0:T(8,128)(2,1)S(1)}, u32[]{:S(2)}, u32[]{:S(2)}) %all-to-all-start.1) | async-done | bytes 147488 | tf_op jit(solution)/shard_map/all_to_all | solution.py:293
  17.8 3.7 %all-to-all-start = ((bf16[8,32,1536]{2,1,0:T(8,128)(2,1)}), bf16[8,32,1536]{2,1,0:T(8,128)(2,1)S(1)}, u32[]{:S(2)}, u32[]{:S(2)}) async-start(bf16[8,32,1536]{2,1,0:T(8,128)(2,1)} %shard_map.73), calls=%async_computation | async-start | bytes 1572864 | tf_op jit(solution)/shard_map/all_to_all | solution.py:298
  21.5 1.5 %collective-permute-start.2 = (bf16[128,576]{1,0:T(8,128)(2,1)S(1)}, bf16[128,576]{1,0:T(8,128)(2,1)S(1)}, u32[]{:S(2)}, u32[]{:S(2)}) collective-permute-start(bf16[128,576]{1,0:T(8,128)(2,1)S(1)} %bitcast.6), channel_id=1, source_target_pairs={{0,96},{16,152},{1,97},{17,153},{2,98},{18,154},{3,99},{19,155},{4... | collective-permute-start | bytes 442376 | tf_op jit(solution)/shard_map/ppermute | solution.py:38
  22.9 1.0 %collective-permute-start.1 = (bf16[128,576]{1,0:T(8,128)(2,1)S(1)}, bf16[128,576]{1,0:T(8,128)(2,1)S(1)}, u32[]{:S(2)}, u32[]{:S(2)}) collective-permute-start(bf16[128,576]{1,0:T(8,128)(2,1)S(1)} %bitcast.7), channel_id=1, source_target_pairs={{0,64},{16,144},{1,65},{17,145},{2,66},{18,146},{3,67},{19,147},{4... | collective-permute-start | bytes 442376 | tf_op jit(solution)/shard_map/ppermute | solution.py:38
  23.9 0.6 dynamic_slice.3
  25.2 0.5 collective-permute-done.3.refs_3_
  25.6 1.3 %collective-permute-done.2.refs_2_ = bf16[128,576]{1,0:T(8,128)(2,1)S(1)} collective-permute-done((bf16[128,576]{1,0:T(8,128)(2,1)S(1)}, bf16[128,576]{1,0:T(8,128)(2,1)S(1)}, u32[]{:S(2)}, u32[]{:S(2)}) %collective-permute-start.2) | collective-permute-done | bytes 147488 | tf_op jit(solution)/shard_map/ppermute | solution.py:38
  26.9 1.7 %collective-permute-done.1.refs_1_ = bf16[128,576]{1,0:T(8,128)(2,1)S(1)} collective-permute-done((bf16[128,576]{1,0:T(8,128)(2,1)S(1)}, bf16[128,576]{1,0:T(8,128)(2,1)S(1)}, u32[]{:S(2)}, u32[]{:S(2)}) %collective-permute-start.1) | collective-permute-done | bytes 147488 | tf_op jit(solution)/shard_map/ppermute | solution.py:38
  28.7 0.2 shard_map.75.rest_0_
  28.9 0.3 collective-permute-start.7
  29.2 1.9 %collective-permute-start.6 = (bf16[4,576,128]{2,1,0:T(8,128)(2,1)S(1)}, bf16[4,576,128]{2,1,0:T(8,128)(2,1)S(1)}, u32[]{:S(2)}, u32[]{:S(2)}) collective-permute-start(bf16[4,576,128]{2,1,0:T(8,128)(2,1)S(1)} %shard_map.75.rest_0_), channel_id=1, source_target_pairs={{0,136},{16,112},{1,137},{17,113},{2,138},{18,114},{3,139},{19,115... | collective-permute-start | bytes 1769480 | tf_op jit(solution)/shard_map/ppermute | solution.py:38
  31.1 6.5 %collective-permute-start.4 = (bf16[4,576,128]{2,1,0:T(8,128)(2,1)S(1)}, bf16[4,576,128]{2,1,0:T(8,128)(2,1)}, u32[]{:S(2)}, u32[]{:S(2)}) collective-permute-start(bf16[4,576,128]{2,1,0:T(8,128)(2,1)S(1)} %shard_map.75.rest_0_), channel_id=1, source_target_pairs={{0,16},{16,0},{1,17},{17,1},{2,18},{18,2},{3,19},{19,3},{4,20},{20... | collective-permute-start | bytes 1769480 | tf_op jit(solution)/shard_map/ppermute | solution.py:38
  37.7 0.6 fusion.2
  38.3 0.2 multiply_sine_fusion
  38.5 4.2 %all-to-all-done.q_ref = bf16[8,32,1536]{2,1,0:T(8,128)(2,1)S(1)} async-done(((bf16[8,32,1536]{2,1,0:T(8,128)(2,1)}), bf16[8,32,1536]{2,1,0:T(8,128)(2,1)S(1)}, u32[]{:S(2)}, u32[]{:S(2)}) %all-to-all-start) | async-done | bytes 786464 | tf_op jit(solution)/shard_map/all_to_all | solution.py:298
  42.7 1.7 %copy-done = bf16[1536,768]{1,0:T(8,128)(2,1)S(1)} copy-done((bf16[1536,768]{1,0:T(8,128)(2,1)S(1)}, bf16[1536,768]{1,0:T(8,128)(2,1)}, u32[]{:S(2)}) %copy-start) | copy-done | bytes 2359320
  44.4 1.0 %copy-done.2 = bf16[4,128,512]{2,1,0:T(8,128)(2,1)S(1)} copy-done((bf16[4,128,512]{2,1,0:T(8,128)(2,1)S(1)}, bf16[4,128,512]{2,1,0:T(8,128)(2,1)}, u32[]{:S(2)}) %copy-start.2) | copy-done | bytes 524312
  45.5 2.3 %shard_map.74.q_ref = bf16[2,576,512]{2,1,0:T(8,128)(2,1)S(1)} custom-call(s32[3]{0:T(128)S(1)} %pad_add_fusion.place_ref, bf16[8,32,1536]{2,1,0:T(8,128)(2,1)S(1)} %all-to-all-done.q_ref, bf16[1,1536]{1,0:T(2,128)(2,1)S(1)} %reshape.23.gain_ref, f32[32,256]{1,0:T(8,128)S(1)} %get-tuple-element.12.cos_ref, f32[32,256]{1,0:T(8,128)S(1)} %get-tuple-element.11.sin_ref, ...), custom_call_target="tpu_custom_call" | custom-call | flops 750000000 | bytes 5000000 | tf_op jit(solution)/shard_map/pallas_call | solution.py:317
  47.8 3.4 %shard_map.76 = (f32[2,512,512]{2,1,0:T(8,128)S(1)}, f32[2,1,512]{2,1,0:T(1,128)S(1)}, f32[2,1,512]{2,1,0:T(1,128)S(1)}) custom-call(s32[3]{0:T(128)S(1)} %pad_add_fusion.place_ref, s32[16]{0:T(128)S(1)} %copy-done.4, bf16[2,576,512]{2,1,0:T(8,128)(2,1)S(1)} %shard_map.74.q_ref, bf16[4,576,128]{2,1,0:T(8,128)(2,1)S(1)} %shard_map.75.rest_0_, ...), custom_call_target="tpu_custom_call" | custom-call | flops 8000000 | bytes 8000 | tf_op jit(solution)/shard_map/pallas_call | solution.py:265
  51.2 3.8 %collective-permute-start.8 = (bf16[4,576,128]{2,1,0:T(8,128)(2,1)S(1)}, bf16[4,576,128]{2,1,0:T(8,128)(2,1)S(1)}, u32[]{:S(2)}, u32[]{:S(2)}) collective-permute-start(bf16[4,576,128]{2,1,0:T(8,128)(2,1)S(1)} %shard_map.77.rest_4_), channel_id=1, source_target_pairs={{0,16},{16,0},{1,17},{17,1},{2,18},{18,2},{3,19},{19,3},{4,20},{20... | collective-permute-start | bytes 1769480 | tf_op jit(solution)/shard_map/ppermute | solution.py:38
  55.0 0.1 collective-permute-start.9
  55.1 0.4 collective-permute-start.10
  55.5 1.1 %collective-permute-done.8.rest_7_ = bf16[4,576,128]{2,1,0:T(8,128)(2,1)S(1)} collective-permute-done((bf16[4,576,128]{2,1,0:T(8,128)(2,1)S(1)}, bf16[4,576,128]{2,1,0:T(8,128)(2,1)S(1)}, u32[]{:S(2)}, u32[]{:S(2)}) %collective-permute-start.8) | collective-permute-done | bytes 589856 | tf_op jit(solution)/shard_map/ppermute | solution.py:38
  56.6 0.8 %collective-permute-done.9.rest_8_ = bf16[4,576,128]{2,1,0:T(8,128)(2,1)S(1)} collective-permute-done((bf16[4,576,128]{2,1,0:T(8,128)(2,1)S(1)}, bf16[4,576,128]{2,1,0:T(8,128)(2,1)S(1)}, u32[]{:S(2)}, u32[]{:S(2)}) %collective-permute-start.9) | collective-permute-done | bytes 589856 | tf_op jit(solution)/shard_map/ppermute | solution.py:38
  57.5 0.8 %collective-permute-done.10.rest_9_ = bf16[4,576,128]{2,1,0:T(8,128)(2,1)S(1)} collective-permute-done((bf16[4,576,128]{2,1,0:T(8,128)(2,1)S(1)}, bf16[4,576,128]{2,1,0:T(8,128)(2,1)S(1)}, u32[]{:S(2)}, u32[]{:S(2)}) %collective-permute-start.10) | collective-permute-done | bytes 589856 | tf_op jit(solution)/shard_map/ppermute | solution.py:38
  58.3 9.7 %shard_map.80 = bf16[256,512]{1,0:T(8,128)(2,1)} custom-call(s32[3]{0:T(128)S(1)} %pad_add_fusion.place_ref, s32[16]{0:T(128)S(1)} %copy-done.4, bf16[2,576,512]{2,1,0:T(8,128)(2,1)S(1)} %shard_map.74.q_ref, bf16[4,512,128]{2,1,0:T(8,128)(2,1)S(1)} %copy-done.1, f32[2,512,512]{2,1,0:T(8,128)S(1)} %get-tuple-element.8.rest_1_, ...), custom_call_target="tpu_custom_call" | custom-call | flops 24000000 | bytes 24000 | tf_op jit(solution)/shard_map/pallas_call | solution.py:265
  (21 shorter events, 0.1 us)
Async XLA Ops:
  0.0 23.9 %copy-start.5 = (bf16[1536]{0:T(1024)(128)(2,1)S(1)}, bf16[1536]{0:T(1024)(128)(2,1)}, u32[]{:S(2)}) copy-start(bf16[1536]{0:T(1024)(128)(2,1)} %param.8) | copy-start | bytes 9220
  0.0 23.9 %copy-start.4 = (s32[16]{0:T(128)S(1)}, s32[16]{0:T(128)}, u32[]{:S(2)}) copy-start(s32[16]{0:T(128)} %owner_ref.3) | copy-start | bytes 196
  1.4 16.3 %all-to-all-start.1 = ((bf16[8,16,576]{2,1,0:T(8,128)(2,1)}), bf16[8,16,576]{2,1,0:T(8,128)(2,1)S(1)}, u32[]{:S(2)}, u32[]{:S(2)}) async-start(bf16[8,16,576]{2,1,0:T(8,128)(2,1)} %broadcast_in_dim.18), calls=%async_computation.1 | async-start | bytes 327680 | tf_op jit(solution)/shard_map/all_to_all | solution.py:293
  9.6 3.2 %collective-permute-start = (bf16[16,1536]{1,0:T(8,128)(2,1)}, bf16[16,1536]{1,0:T(8,128)(2,1)S(1)}, u32[]{:S(2)}, u32[]{:S(2)}) collective-permute-start(bf16[16,1536]{1,0:T(8,128)(2,1)} %q_ref.1), channel_id=1, source_target_pairs={{0,8},{16,24},{1,9},{17,25},{2,10},{18,26},{3,11},{19,27},{4,12},{... | collective-permute-start | bytes 147464 | tf_op jit(solution)/shard_map/ppermute | solution.py:38
  12.8 0.8 %copy-start.3 = (bf16[16,1536]{1,0:T(8,128)(2,1)S(1)}, bf16[16,1536]{1,0:T(8,128)(2,1)}, u32[]{:S(2)}) copy-start(bf16[16,1536]{1,0:T(8,128)(2,1)} %q_ref.1) | copy-start | bytes 147460
  17.8 25.0 %all-to-all-start = ((bf16[8,32,1536]{2,1,0:T(8,128)(2,1)}), bf16[8,32,1536]{2,1,0:T(8,128)(2,1)S(1)}, u32[]{:S(2)}, u32[]{:S(2)}) async-start(bf16[8,32,1536]{2,1,0:T(8,128)(2,1)} %shard_map.73), calls=%async_computation | async-start | bytes 1572864 | tf_op jit(solution)/shard_map/all_to_all | solution.py:298
  21.5 4.2 %collective-permute-start.3 = (bf16[128,576]{1,0:T(8,128)(2,1)S(1)}, bf16[128,576]{1,0:T(8,128)(2,1)S(1)}, u32[]{:S(2)}, u32[]{:S(2)}) collective-permute-start(bf16[128,576]{1,0:T(8,128)(2,1)S(1)} %bitcast.5), channel_id=1, source_target_pairs={{0,32},{16,24},{1,33},{17,25},{2,34},{18,26},{3,35},{19,27},{4,36}... | collective-permute-start | bytes 442376 | tf_op jit(solution)/shard_map/ppermute | solution.py:38
  21.5 5.5 %collective-permute-start.2 = (bf16[128,576]{1,0:T(8,128)(2,1)S(1)}, bf16[128,576]{1,0:T(8,128)(2,1)S(1)}, u32[]{:S(2)}, u32[]{:S(2)}) collective-permute-start(bf16[128,576]{1,0:T(8,128)(2,1)S(1)} %bitcast.6), channel_id=1, source_target_pairs={{0,96},{16,152},{1,97},{17,153},{2,98},{18,154},{3,99},{19,155},{4... | collective-permute-start | bytes 442376 | tf_op jit(solution)/shard_map/ppermute | solution.py:38
  22.9 5.8 %collective-permute-start.1 = (bf16[128,576]{1,0:T(8,128)(2,1)S(1)}, bf16[128,576]{1,0:T(8,128)(2,1)S(1)}, u32[]{:S(2)}, u32[]{:S(2)}) collective-permute-start(bf16[128,576]{1,0:T(8,128)(2,1)S(1)} %bitcast.7), channel_id=1, source_target_pairs={{0,64},{16,144},{1,65},{17,145},{2,66},{18,146},{3,67},{19,147},{4... | collective-permute-start | bytes 442376 | tf_op jit(solution)/shard_map/ppermute | solution.py:38
  28.9 26.2 %collective-permute-start.7 = (bf16[4,576,128]{2,1,0:T(8,128)(2,1)S(1)}, bf16[4,576,128]{2,1,0:T(8,128)(2,1)S(1)}, u32[]{:S(2)}, u32[]{:S(2)}) collective-permute-start(bf16[4,576,128]{2,1,0:T(8,128)(2,1)S(1)} %shard_map.75.rest_0_), channel_id=1, source_target_pairs={{0,128},{16,80},{1,129},{17,81},{2,130},{18,82},{3,131},{19,83},{4... | collective-permute-start | bytes 1769480 | tf_op jit(solution)/shard_map/ppermute | solution.py:38
  29.2 25.8 %collective-permute-start.6 = (bf16[4,576,128]{2,1,0:T(8,128)(2,1)S(1)}, bf16[4,576,128]{2,1,0:T(8,128)(2,1)S(1)}, u32[]{:S(2)}, u32[]{:S(2)}) collective-permute-start(bf16[4,576,128]{2,1,0:T(8,128)(2,1)S(1)} %shard_map.75.rest_0_), channel_id=1, source_target_pairs={{0,136},{16,112},{1,137},{17,113},{2,138},{18,114},{3,139},{19,115... | collective-permute-start | bytes 1769480 | tf_op jit(solution)/shard_map/ppermute | solution.py:38
  31.1 20.1 %collective-permute-start.5 = (bf16[4,576,128]{2,1,0:T(8,128)(2,1)S(1)}, bf16[4,576,128]{2,1,0:T(8,128)(2,1)S(1)}, u32[]{:S(2)}, u32[]{:S(2)}) collective-permute-start(bf16[4,576,128]{2,1,0:T(8,128)(2,1)S(1)} %shard_map.75.rest_0_), channel_id=1, source_target_pairs={{0,8},{16,48},{1,9},{17,49},{2,10},{18,50},{3,11},{19,51},{4,12},{... | collective-permute-start | bytes 1769480 | tf_op jit(solution)/shard_map/ppermute | solution.py:38
  31.1 16.7 %collective-permute-start.4 = (bf16[4,576,128]{2,1,0:T(8,128)(2,1)S(1)}, bf16[4,576,128]{2,1,0:T(8,128)(2,1)}, u32[]{:S(2)}, u32[]{:S(2)}) collective-permute-start(bf16[4,576,128]{2,1,0:T(8,128)(2,1)S(1)} %shard_map.75.rest_0_), channel_id=1, source_target_pairs={{0,16},{16,0},{1,17},{17,1},{2,18},{18,2},{3,19},{19,3},{4,20},{20... | collective-permute-start | bytes 1769480 | tf_op jit(solution)/shard_map/ppermute | solution.py:38
  42.7 1.7 %copy-start = (bf16[1536,768]{1,0:T(8,128)(2,1)S(1)}, bf16[1536,768]{1,0:T(8,128)(2,1)}, u32[]{:S(2)}) copy-start(bf16[1536,768]{1,0:T(8,128)(2,1)} %up_ref.1) | copy-start | bytes 7077892
  44.4 1.0 %copy-start.2 = (bf16[4,128,512]{2,1,0:T(8,128)(2,1)S(1)}, bf16[4,128,512]{2,1,0:T(8,128)(2,1)}, u32[]{:S(2)}) copy-start(bf16[4,128,512]{2,1,0:T(8,128)(2,1)} %ak_ref.1) | copy-start | bytes 1572868
  51.2 7.1 %copy-start.1 = (bf16[4,512,128]{2,1,0:T(8,128)(2,1)S(1)}, bf16[4,512,128]{2,1,0:T(8,128)(2,1)}, u32[]{:S(2)}) copy-start(bf16[4,512,128]{2,1,0:T(8,128)(2,1)} %rest_0_.1) | copy-start | bytes 1572868
  51.2 5.4 %collective-permute-start.8 = (bf16[4,576,128]{2,1,0:T(8,128)(2,1)S(1)}, bf16[4,576,128]{2,1,0:T(8,128)(2,1)S(1)}, u32[]{:S(2)}, u32[]{:S(2)}) collective-permute-start(bf16[4,576,128]{2,1,0:T(8,128)(2,1)S(1)} %shard_map.77.rest_4_), channel_id=1, source_target_pairs={{0,16},{16,0},{1,17},{17,1},{2,18},{18,2},{3,19},{19,3},{4,20},{20... | collective-permute-start | bytes 1769480 | tf_op jit(solution)/shard_map/ppermute | solution.py:38
  55.0 2.5 %collective-permute-start.9 = (bf16[4,576,128]{2,1,0:T(8,128)(2,1)S(1)}, bf16[4,576,128]{2,1,0:T(8,128)(2,1)S(1)}, u32[]{:S(2)}, u32[]{:S(2)}) collective-permute-start(bf16[4,576,128]{2,1,0:T(8,128)(2,1)S(1)} %shard_map.78.rest_5_), channel_id=1, source_target_pairs={{0,16},{16,0},{1,17},{17,1},{2,18},{18,2},{3,19},{19,3},{4,20},{20... | collective-permute-start | bytes 1769480 | tf_op jit(solution)/shard_map/ppermute | solution.py:38
  55.1 3.2 %collective-permute-start.10 = (bf16[4,576,128]{2,1,0:T(8,128)(2,1)S(1)}, bf16[4,576,128]{2,1,0:T(8,128)(2,1)S(1)}, u32[]{:S(2)}, u32[]{:S(2)}) collective-permute-start(bf16[4,576,128]{2,1,0:T(8,128)(2,1)S(1)} %shard_map.79.rest_6_), channel_id=1, source_target_pairs={{0,16},{16,0},{1,17},{17,1},{2,18},{18,2},{3,19},{19,3},{4,20},{20... | collective-permute-start | bytes 1769480 | tf_op jit(solution)/shard_map/ppermute | solution.py:38
